TPU v7x, 512 devices: a whole 4x4x16 slice. The times are simulated.
512 devices in a mesh: seq: 8 (over y, core), head: 64 (over z, x).
Axes of the slice: x: 4, y: 4, z: 16, core: 2. Of those that a mesh axis runs over, the one named last changes fastest.
Arguments:
- tokens: bfloat16 [8192, 2048], P('seq', 'head'), may hold values from -6 to 6
- z_weight: bfloat16 [2048, 4096], P(None, 'head'), may hold values from -0.125 to 0.125
- x_weight: bfloat16 [2048, 4096], P(None, 'head'), may hold values from -0.79549513 to 0.79549513
- bc_weight: bfloat16 [2048, 256], replicated, may hold values from -0.125 to 0.125
- step_weight: bfloat16 [2048, 64], P(None, 'head'), may hold values from -0.125 to 0.125
- x_kernel: float32 [4, 4096], P(None, 'head'), may hold values from -3 to 3
- bc_kernel: float32 [4, 256], replicated, may hold values from -3 to 3
- step_bias: float32 [64], P('head'), may hold values from -9 to -3
- log_decay: float32 [64], P('head'), may hold values from 0 to 1.5
- skip_gain: float32 [64], P('head'), may hold values from 0.2 to 0.8
- norm_gain: bfloat16 [4096], P('head'), may hold values from 0.099609375 to 1.8984375
- out_weight: bfloat16 [4096, 2048], P('head'), may hold values from -0.09375 to 0.09375
Outputs:
- mixed: bfloat16 [8192, 2048], P('seq', 'head')
All inputs are finite; a program needn't handle non-finite values.
Results may differ from a plain program's by a relative error of at most 0.017.
Values may be sent and summed in bfloat16 or wider, within the bound.
A program may use at most 64 MiB of HBM per device.

v0:
```python
import jax
import jax.numpy as jnp
from jax import lax
from jax.sharding import PartitionSpec as P

CH = 256


def from_behind(block, axis, distance):
    devices = range(lax.axis_size(axis))
    route = [(i - distance, i) for i in devices if i - distance in devices]
    return lax.ppermute(block, axis, route)


def causal(padded, kernel):
    length = padded.shape[0] - 3
    total = kernel[0] * padded[0:length].astype(jnp.float32)
    for offset in range(1, 4):
        total = total + kernel[offset] * padded[offset : offset + length].astype(jnp.float32)
    return jax.nn.silu(total).astype(jnp.bfloat16)


def body(
    tokens,
    z_weight,
    x_weight,
    bc_weight,
    step_weight,
    x_kernel,
    bc_kernel,
    step_bias,
    log_decay,
    skip_gain,
    norm_gain,
    out_weight,
):
    tok_rows = tokens.shape[0]
    heads_here = step_bias.shape[0]
    inner_width = x_weight.shape[1]
    head_size = inner_width // heads_here
    state_size = bc_weight.shape[1] // 2
    piece = lax.all_gather(tokens, "head", axis=1, tiled=True)

    def product(weight):
        return jnp.dot(piece, weight, preferred_element_type=jnp.float32)

    z_sum = product(z_weight)
    x_sum = product(x_weight)
    bc_sum = product(bc_weight)
    step_raw = product(step_weight)
    z_in = z_sum.astype(jnp.bfloat16)
    x_in = x_sum.astype(jnp.bfloat16)
    bc_in = bc_sum.astype(jnp.bfloat16)
    border = jnp.concatenate([x_in[-3:], bc_in[-3:]], axis=1)
    border = from_behind(border, "seq", 1)
    x_conv = causal(jnp.concatenate([border[:, :inner_width], x_in], axis=0), x_kernel)
    bc_conv = causal(jnp.concatenate([border[:, inner_width:], bc_in], axis=0), bc_kernel)
    blocks = tok_rows // CH
    b_map = bc_conv[:, :state_size].reshape(blocks, CH, state_size)
    c_map = bc_conv[:, state_size:].reshape(blocks, CH, state_size)
    step_size = jax.nn.softplus(step_raw + step_bias)
    rate = -jnp.exp(log_decay) * step_size
    values = x_conv.reshape(blocks, CH, heads_here, head_size)
    steps_b = step_size.reshape(blocks, CH, heads_here)
    cumulative = jnp.cumsum(rate.reshape(blocks, CH, heads_here), axis=1)
    lower = (jnp.arange(CH)[:, None] >= jnp.arange(CH)[None, :])[None, :, :, None]
    gram = jnp.einsum("ctn,csn->cts", c_map, b_map, preferred_element_type=jnp.float32)
    spread = cumulative[:, :, None, :] - cumulative[:, None, :, :]
    mixing = jnp.where(
        lower,
        gram[..., None] * jnp.exp(jnp.where(lower, spread, 0.0)) * steps_b[:, None, :, :],
        0.0,
    ).astype(jnp.bfloat16)
    intra = jnp.einsum("ctsh,cshp->cthp", mixing, values, preferred_element_type=jnp.float32)
    tails = jnp.exp(cumulative[:, -1:, :] - cumulative) * steps_b
    weighted = (values.astype(jnp.float32) * tails[..., None]).astype(jnp.bfloat16)
    local = jnp.einsum("cthp,ctn->chpn", weighted, b_map, preferred_element_type=jnp.float32)
    block_decay = jnp.exp(cumulative[:, -1, :])

    def advance(carry, item):
        state, decay = carry
        term, factor = item
        return ((factor[:, None, None] * state + term, decay * factor), (state, decay))

    zero_state = jnp.zeros((heads_here, head_size, state_size), jnp.float32)
    unit_decay = jnp.ones((heads_here,), jnp.float32)
    (shard_state, shard_decay), (local_in, decay_in) = lax.scan(
        advance, (zero_state, unit_decay), (local, block_decay)
    )

    def relay(index, carried):
        return from_behind(shard_decay[:, None, None] * carried + shard_state, "seq", 1)

    incoming = lax.fori_loop(0, lax.axis_size("seq") - 1, relay, zero_state)
    entering = local_in + decay_in[:, :, None, None] * incoming[None]
    held = entering.astype(jnp.bfloat16)
    from_state = (
        jnp.einsum("ctn,chpn->cthp", c_map, held, preferred_element_type=jnp.float32)
        * jnp.exp(cumulative)[..., None]
    )
    output_y = intra + from_state + skip_gain[None, None, :, None] * values.astype(jnp.float32)
    gated = (
        output_y.reshape(tok_rows, inner_width) * jax.nn.silu(z_in.astype(jnp.float32))
    ).astype(jnp.bfloat16)
    head_count = lax.axis_size("head")
    columns = lax.all_to_all(out_weight, "head", split_axis=1, concat_axis=0, tiled=True)
    gain_row = norm_gain.reshape(1, inner_width)
    section = lax.all_gather(gated, "head", axis=1, tiled=True)
    gain_part = lax.all_gather(gain_row, "head", axis=1, tiled=True)
    section_f = section.astype(jnp.float32)
    scaled = (section_f * gain_part.astype(jnp.float32)).astype(jnp.bfloat16)
    partial_out = jnp.dot(scaled, columns, preferred_element_type=jnp.float32)
    squares = jnp.sum(section_f * section_f, axis=1)
    meansq = squares / (inner_width * head_count)
    return (partial_out * lax.rsqrt(meansq + 1e-05)[:, None]).astype(jnp.bfloat16)


def solution(mesh):
    placed = (
        P("seq", "head"),
        P(None, "head"),
        P(None, "head"),
        P(),
        P(None, "head"),
        P(None, "head"),
        P(),
        P("head"),
        P("head"),
        P("head"),
        P("head"),
        P("head", None),
    )
    return jax.shard_map(
        body, mesh=mesh, in_specs=placed, out_specs=P("seq", "head"), check_vma=False
    )
```

profile of v0, /device:TPU:10, one launch (start us, length us, event | category | flops | bytes accessed | tf_op | source)
XLA Modules:
  0.0 403.9 jit_solution(2700277313001061849)
XLA Ops:
  6.5 0.7 all-gather.4.cloned.1.call-update
  9.4 0.8 slice_bitcast_fusion.4
  10.2 0.8 fusion.44
  11.0 148.9 %all-gather.4.cloned.1.call-done = bf16[1024,2048]{0,1:T(8,128)(2,1)} async-done(((bf16[1024,32]{0,1:T(8,128)(2,1)}), bf16[1024,2048]{0,1:T(8,128)(2,1)}) %all-gather.4.cloned.1.call-update) | async-done | bytes 4194320 | tf_op jit(solution)/shard_map/all_gather | solution.py:42
  160.0 2.8 fusion.45
  162.8 1.2 reduce-window.6
  164.3 3.6 convolution_convert_fusion
  168.0 0.9 convolution_convert_fusion.2
  169.0 1.9 collective-permute-start.1
  171.3 3.5 collective-permute-done.1
  174.8 1.0 multiply_convert_fusion
  176.2 0.3 convert_multiply_fusion.2
  176.8 8.1 %while.28 = (s32[]{:T(128)}, f32[1,64,128]{2,1,0:T(8,128)S(1)}, f32[1]{0:T(128)}, f32[4,1,64,128]{3,2,1,0:T(8,128)S(1)}, f32[4,1]{0,1:T(1,128)S(1)}, /*index=5*/...) while((s32[]{:T(128)}, f32[1,64,128]{2,1,0:T(8,128)S(1)}, f32[1]{0:T(128)}, ...), condition=%wide.region_3.4_spmd.clone, body=%wide.region_2.3_spmd.clone.sunk | while | flops 32772 | bytes 164008 | solution.py:87
  176.8 0.6 constant_dynamic-slice_fusion.2
  177.4 0.7 bitcast_add_fusion.4
  178.8 0.6 constant_dynamic-slice_fusion.2
  179.4 0.7 bitcast_add_fusion.4
  180.8 0.6 constant_dynamic-slice_fusion.2
  181.4 0.7 bitcast_add_fusion.4
  182.8 0.6 constant_dynamic-slice_fusion.2
  183.4 0.7 bitcast_add_fusion.4
  184.8 0.5 fusion.10
  185.4 36.8 %while.27 = (s32[]{:T(128)}, f32[1,64,128]{2,1,0:T(8,128)S(1)}, f32[1]{0:T(128)}, f32[1,64,128]{2,1,0:T(8,128)S(1)}, s32[]{:T(128)}) while((s32[]{:T(128)}, f32[1,64,128]{2,1,0:T(8,128)S(1)}, f32[1]{0:T(128)}, f32[1,64,128]{2,1,0:T(8,128)S(1)}, s32[]{:T(128)}) %tuple.53), condition=%wide.region_5.6_spmd, body=%wide.region_4.5_spmd.sunk | while | flops 16386 | bytes 229481 | solution.py:94
  185.4 2.1 collective-permute-start
  187.5 3.3 collective-permute-done
  190.8 1.9 collective-permute-start
  192.7 3.3 collective-permute-done
  196.0 1.9 collective-permute-start
  198.0 3.3 collective-permute-done
  201.3 1.9 collective-permute-start
  203.2 3.3 collective-permute-done
  206.5 1.9 collective-permute-start
  208.4 3.3 collective-permute-done
  211.7 1.9 collective-permute-start
  213.7 3.3 collective-permute-done
  217.0 1.9 collective-permute-start
  218.9 3.3 collective-permute-done
  222.7 3.7 multiply_convert_fusion.1
  226.5 0.3 copy.63
  226.8 1.0 reshape.305
  227.8 10.3 %all-to-all-start = ((bf16[64,2,1024]{2,1,0:T(2,128)(2,1)}), bf16[64,2,1024]{2,1,0:T(2,128)(2,1)S(1)}, u32[]{:S(2)}, u32[]{:S(2)}) async-start(bf16[64,2,1024]{2,1,0:T(2,128)(2,1)} %reshape.305), calls=%async_computation | async-start | bytes 524288 | tf_op jit(solution)/shard_map/all_to_all | solution.py:106
  238.1 1.3 dynamic-slice
  240.3 147.3 %all-reduce = bf16[4096]{0:T(1024)(128)(2,1)S(1)} all-reduce(bf16[4096]{0:T(1024)(128)(2,1)S(1)} %dynamic-update-slice), channel_id=2, replica_groups=mesh['seq'=8,'head'=64] {'head'}, use_global_device_ids=true, to_apply=%add | all-reduce | flops 4096 | bytes 16384
  387.6 0.3 reshape.306
  388.2 0.5 all_to_all.17
  388.7 5.2 %fusion.1 = f32[1024]{0:T(1024)S(1)} fusion(bf16[1024,4096]{0,1:T(8,128)(2,1)} %all-gather.6.cloned.1.call-done), kind=kLoop, calls=%fused_computation.7 | loop fusion | flops 12581888 | bytes 8392704 | tf_op jit(solution)/shard_map/reduce_sum | solution.py:113
  394.0 0.5 copy-done.2
  394.5 2.5 fusion.17
  (69 shorter events, 3.0 us)
Async XLA Ops:
  6.5 157.7 %copy-start = (bf16[2048,256]{1,0:T(8,128)(2,1)S(1)}, bf16[2048,256]{1,0:T(8,128)(2,1)}, u32[]{:S(2)}) copy-start(bf16[2048,256]{1,0:T(8,128)(2,1)} %param.19) | copy-start | bytes 3145732
  6.5 153.4 %all-gather.4.cloned.1.call-start = ((), (), s32[]{:S(2)}) async-start(), calls=%async_computation.1 | async-start | bytes 4259840 | tf_op jit(solution)/shard_map/all_gather | solution.py:42
  7.3 381.4 %all-gather.6.cloned.1.call-start = ((), (), s32[]{:S(2)}) async-start(), calls=%async_computation.2 | async-start | bytes 8519680 | tf_op jit(solution)/shard_map/all_gather | solution.py:108
  164.3 3.8 copy-start.1
  164.3 3.8 copy-start.3
  169.0 5.8 %collective-permute-start.1 = (bf16[3,320]{0,1:T(8,128)(2,1)S(1)}, bf16[3,320]{0,1:T(8,128)(2,1)S(1)}, u32[]{:S(2)}, u32[]{:S(2)}) collective-permute-start(bf16[3,320]{0,1:T(8,128)(2,1)S(1)} %pad_maximum_fusion.2), channel_id=1, source_target_pairs={{0,64},{64,128},{128,192},{192,256},{256,320},{320,384},{384,448},... | collective-permute-start | bytes 5768 | tf_op jit(solution)/shard_map/ppermute | solution.py:12
  176.2 46.5 %copy-start.4 = (bf16[2048,64]{0,1:T(8,128)(2,1)S(1)}, bf16[2048,64]{0,1:T(8,128)(2,1)}, u32[]{:S(2)}) copy-start(bf16[2048,64]{0,1:T(8,128)(2,1)} %param.17) | copy-start | bytes 786436
  185.4 41.1 %copy-start.5 = (bf16[64,2048]{1,0:T(8,128)(2,1)S(1)}, bf16[64,2048]{1,0:T(8,128)(2,1)}, u32[]{:S(2)}) copy-start(bf16[64,2048]{1,0:T(8,128)(2,1)} %param.27) | copy-start | bytes 786436
  185.4 5.4 %collective-permute-start = (f32[1,64,128]{2,1,0:T(8,128)S(1)}, f32[1,64,128]{2,1,0:T(8,128)S(1)}, u32[]{:S(2)}, u32[]{:S(2)}) collective-permute-start(f32[1,64,128]{2,1,0:T(8,128)S(1)} %multiply_add_fusion.2), channel_id=1, source_target_pairs={{0,64},{64,128},{128,192},{192,256},{256,320},{320,384},{384,448},... | collective-permute-start | bytes 98312 | tf_op jit(solution)/shard_map/while/body/eval_jaxpr/ppermute | solution.py:12
  190.8 5.2 %collective-permute-start = (f32[1,64,128]{2,1,0:T(8,128)S(1)}, f32[1,64,128]{2,1,0:T(8,128)S(1)}, u32[]{:S(2)}, u32[]{:S(2)}) collective-permute-start(f32[1,64,128]{2,1,0:T(8,128)S(1)} %multiply_add_fusion.2), channel_id=1, source_target_pairs={{0,64},{64,128},{128,192},{192,256},{256,320},{320,384},{384,448},... | collective-permute-start | bytes 98312 | tf_op jit(solution)/shard_map/while/body/eval_jaxpr/ppermute | solution.py:12
  196.0 5.2 %collective-permute-start = (f32[1,64,128]{2,1,0:T(8,128)S(1)}, f32[1,64,128]{2,1,0:T(8,128)S(1)}, u32[]{:S(2)}, u32[]{:S(2)}) collective-permute-start(f32[1,64,128]{2,1,0:T(8,128)S(1)} %multiply_add_fusion.2), channel_id=1, source_target_pairs={{0,64},{64,128},{128,192},{192,256},{256,320},{320,384},{384,448},... | collective-permute-start | bytes 98312 | tf_op jit(solution)/shard_map/while/body/eval_jaxpr/ppermute | solution.py:12
  201.3 5.2 %collective-permute-start = (f32[1,64,128]{2,1,0:T(8,128)S(1)}, f32[1,64,128]{2,1,0:T(8,128)S(1)}, u32[]{:S(2)}, u32[]{:S(2)}) collective-permute-start(f32[1,64,128]{2,1,0:T(8,128)S(1)} %multiply_add_fusion.2), channel_id=1, source_target_pairs={{0,64},{64,128},{128,192},{192,256},{256,320},{320,384},{384,448},... | collective-permute-start | bytes 98312 | tf_op jit(solution)/shard_map/while/body/eval_jaxpr/ppermute | solution.py:12
  206.5 5.2 %collective-permute-start = (f32[1,64,128]{2,1,0:T(8,128)S(1)}, f32[1,64,128]{2,1,0:T(8,128)S(1)}, u32[]{:S(2)}, u32[]{:S(2)}) collective-permute-start(f32[1,64,128]{2,1,0:T(8,128)S(1)} %multiply_add_fusion.2), channel_id=1, source_target_pairs={{0,64},{64,128},{128,192},{192,256},{256,320},{320,384},{384,448},... | collective-permute-start | bytes 98312 | tf_op jit(solution)/shard_map/while/body/eval_jaxpr/ppermute | solution.py:12
  211.7 5.2 %collective-permute-start = (f32[1,64,128]{2,1,0:T(8,128)S(1)}, f32[1,64,128]{2,1,0:T(8,128)S(1)}, u32[]{:S(2)}, u32[]{:S(2)}) collective-permute-start(f32[1,64,128]{2,1,0:T(8,128)S(1)} %multiply_add_fusion.2), channel_id=1, source_target_pairs={{0,64},{64,128},{128,192},{192,256},{256,320},{320,384},{384,448},... | collective-permute-start | bytes 98312 | tf_op jit(solution)/shard_map/while/body/eval_jaxpr/ppermute | solution.py:12
  217.0 5.2 %collective-permute-start = (f32[1,64,128]{2,1,0:T(8,128)S(1)}, f32[1,64,128]{2,1,0:T(8,128)S(1)}, u32[]{:S(2)}, u32[]{:S(2)}) collective-permute-start(f32[1,64,128]{2,1,0:T(8,128)S(1)} %multiply_add_fusion.2), channel_id=1, source_target_pairs={{0,64},{64,128},{128,192},{192,256},{256,320},{320,384},{384,448},... | collective-permute-start | bytes 98312 | tf_op jit(solution)/shard_map/while/body/eval_jaxpr/ppermute | solution.py:12
  222.4 17.6 %copy-start.6 = (bf16[64]{0:T(256)(128)(2,1)S(1)}, bf16[64]{0:T(256)(128)(2,1)}, u32[]{:S(2)}) copy-start(bf16[64]{0:T(256)(128)(2,1)} %param.26) | copy-start | bytes 388
  227.8 159.8 %all-to-all-start = ((bf16[64,2,1024]{2,1,0:T(2,128)(2,1)}), bf16[64,2,1024]{2,1,0:T(2,128)(2,1)S(1)}, u32[]{:S(2)}, u32[]{:S(2)}) async-start(bf16[64,2,1024]{2,1,0:T(2,128)(2,1)} %reshape.305), calls=%async_computation | async-start | bytes 524288 | tf_op jit(solution)/shard_map/all_to_all | solution.py:106
  388.7 5.8 %copy-start.2 = (bf16[1024,4096]{0,1:T(8,128)(2,1)S(1)}, bf16[1024,4096]{0,1:T(8,128)(2,1)}, u32[]{:S(2)}) copy-start(bf16[1024,4096]{0,1:T(8,128)(2,1)} %all-gather.6.cloned.1.call-done) | copy-start | bytes 25165828
Sparse Core Ops, SparseCore 0:
  10.3 149.6 all-gather.3
  226.6 154.3 all-gather.5
where the time goes:
time: 404 us
  waiting for transfers between devices  176 us (44%)
  blocking collectives  147 us (36%)
  starting transfers between devices  25.8 us (6%)
  between operations  16.4 us (4%)
  matrix products  14.6 us (4%)
  other arithmetic  10.6 us (3%)
  local copies, waits for them, and re-layouts  10.1 us (2%)
    all_gather x1, waiting for transfers between devices, body(): piece = lax.all_gather(tokens, 'head', axis=1, tiled=True)  149 us
    unnamed x1, blocking collectives  147 us
    ppermute x8, waiting for transfers between devices, from_behind(): return lax.ppermute(block, axis, route)  26.6 us
    ppermute x8, starting transfers between devices, from_behind(): return lax.ppermute(block, axis, route)  15.4 us
    dot_general x4, matrix products, product(): return jnp.dot(piece, weight, preferred_element_type=jnp.float32)  11.1 us
    all_to_all x1, starting transfers between devices, body(): lax.all_to_all(out_weight, 'head', split_axis=1, concat_axis=0, tiled=True)  10.3 us
  transfers between devices with their start and end apart: 11, of which 9 were waited for; matrix products, arithmetic and copies ran while one was open for 1% of the time, Pallas kernels for 0%

commit v1 on v0

v1 whole, which is shorter than its diff:
```python
import functools

import jax
import jax.numpy as jnp
from jax import lax
from jax.experimental import pallas as pl
from jax.experimental.pallas import tpu as pltpu
from jax.sharding import PartitionSpec as P

MESH = pl.DeviceIdType.MESH
F32 = jnp.float32
BF16 = jnp.bfloat16
NX = 4
BLK = 256
NONE = (((1,), (0,)), ((), ()))
BOTH = (((1,), (1,)), ((), ()))


def dot(a, b, dims=NONE):
    return lax.dot_general(a, b, dims, preferred_element_type=F32)


def kernel(
    ns,
    nz,
    tok_in,
    zw_in,
    xw_in,
    bcw_in,
    sw_in,
    xk_in,
    bck_in,
    bias_in,
    decay_in,
    skip_in,
    gain_in,
    ow_in,
    out_ref,
    tok,
    zw,
    xw,
    bcw,
    bct,
    ow,
    owt,
    par,
    swf,
    pt,
    ptt,
    ct,
    xin,
    zsil,
    xc,
    halo_s,
    halo_r,
    tr,
    bcv,
    wt,
    yv,
    st1s,
    st1r,
    st2s,
    st2r,
    hs,
    held,
    sqs,
    sqr,
    sc,
    rs_rs,
    rs_ls,
    rs_rr,
    rs_lr,
    res,
    lsem,
    p1s,
    p1r,
    ws,
    wr,
    sibs,
    sibr,
    ps,
    pr,
    ags,
    agr,
    hsem,
    s1s,
    s1r,
    s2s,
    s2r,
    s3s,
    s3r,
    sqss,
    sqrs,
    rss,
    rsr,
    p4s,
    p4r,
):
    half = nz // 2
    width = 128 * nz
    s = lax.axis_index("seq")
    h = lax.axis_index("head")
    z = h // NX
    x = lax.rem(h, NX)
    core = lax.rem(s, 2)
    block = s * NX + x
    blocks = ns * NX

    def at(s_to, z_to, x_to):
        return (s_to, z_to * NX + x_to)

    def mod(v, n):
        return lax.rem(v + n, n)

    right = at(s, mod(z + 1, nz), x)
    left = at(s, mod(z - 1, nz), x)
    x_up = at(s, z, mod(x + 1, NX))
    x_down = at(s, z, mod(x - 1, NX))
    sibling = (s + 1 - 2 * core, h)
    after = mod(block + 1, blocks)
    before = mod(block - 1, blocks)
    next_dev = at(after // NX, z, lax.rem(after, NX))
    prev_dev = at(before // NX, z, lax.rem(before, NX))

    def remote(src, dst, send, recv, to):
        return pltpu.make_async_remote_copy(
            src_ref=src, dst_ref=dst, send_sem=send, recv_sem=recv, device_id=to, device_id_type=MESH
        )

    def rows(ref, start, count):
        return ref.at[pl.ds(pl.multiple_of(start, count), count)]

    own_tok = rows(tok, 128 * z + 32 * x, 32)
    my_cols = pl.ds(pl.multiple_of(BLK * x, BLK), BLK)
    local = [
        pltpu.make_async_copy(tok_in.at[:, my_cols], own_tok, lsem.at[0]),
        pltpu.make_async_copy(bcw_in, bcw, lsem.at[1]),
        pltpu.make_async_copy(zw_in, rows(zw, 64 * x, 64), lsem.at[2]),
        pltpu.make_async_copy(xw_in, rows(xw, 64 * x, 64), lsem.at[3]),
        pltpu.make_async_copy(ow_in, rows(ow, 64 * x, 64), lsem.at[4]),
    ]
    for c in local:
        c.start()

    barrier = pltpu.get_barrier_semaphore()

    def greet(to):
        pl.semaphore_signal(barrier, inc=1, device_id=to, device_id_type=MESH)

    for d in range(1, NX):
        greet(at(s, z, mod(x + d, NX)))
    for d in range(1, nz):
        greet(at(s, mod(z + d, nz), x))
    for d in range(1, ns):
        greet((mod(s + d, ns), h))
    greet(next_dev)
    greet(prev_dev)

    par[x] = jnp.zeros((24, 128), F32)
    sw = sw_in[...].astype(F32)
    for r in range(nz):
        par[x, r : r + 1, :] = sw[:, 128 * r : 128 * r + 128]
    xk = xk_in[...]
    par[x, 16:20, :] = jnp.concatenate([xk, xk], axis=1)
    gain = gain_in[...].astype(F32)
    par[x, 20:21, :] = jnp.concatenate([gain, gain], axis=1)
    par[x, 21:22, :] = jnp.full((1, 128), bias_in[0], F32)
    par[x, 22:23, :] = jnp.full((1, 128), decay_in[0], F32)
    par[x, 23:24, :] = jnp.full((1, 128), skip_in[0], F32)

    pl.semaphore_wait(barrier, (NX - 1) + (nz - 1) + (ns - 1) + 2)

    p1 = []
    for d in range(1, NX):
        xp = mod(x + d, NX)
        cols = pl.ds(pl.multiple_of(BLK * xp, BLK), BLK)
        c = remote(tok_in.at[:, cols], own_tok, p1s.at[d - 1], p1r.at[d - 1], at(s, z, xp))
        c.start()
        p1.append(c)
    small = []
    for d in range(1, NX):
        c = remote(par.at[x], par.at[x], ps.at[d - 1], pr.at[d - 1], at(s, z, mod(x + d, NX)))
        c.start()
        small.append(c)

    hr = 32 * core

    def wrow(ref, j):
        return rows(ref, 64 * j + hr, 32)

    half_in = pl.ds(pl.multiple_of(hr, 32), 32)
    wx = []
    for n, (src, buf) in enumerate(((zw_in, zw), (xw_in, xw))):
        up = remote(src.at[half_in], wrow(buf, x), ws.at[2 * n], wr.at[2 * n], x_up)
        down = remote(src.at[half_in], wrow(buf, x), ws.at[2 * n + 1], wr.at[2 * n + 1], x_down)
        wx.append((up, down))

    for c in local:
        c.wait()
    for c in p1:
        c.wait_recv()
    wx[1][0].start()
    wx[0][1].start()
    wx[0][0].start()
    wx[1][1].start()

    def ag(k, p, direction):
        src = mod(z - k, nz) if direction == 0 else mod(z + k, nz)
        ref = rows(tok, 128 * src + 64 * p, 64)
        to = right if direction == 0 else left
        return remote(ref, ref, ags.at[direction, k, p], agr.at[direction, k, p], to)

    def ag_wait(k, p, direction):
        src = mod(z - k - 1, nz) if direction == 0 else mod(z + k + 1, nz)
        ref = rows(tok, 128 * src + 64 * p, 64)
        remote(ref, ref, ags.at[direction, k, p], agr.at[direction, k, p], right).wait_recv()

    def transpose_bc(k):
        piece = bcw[pl.ds(pl.multiple_of(BLK * k, BLK), BLK), :]
        bct[:, pl.ds(pl.multiple_of(BLK * k, BLK), BLK)] = piece.T

    for p in range(2):
        for direction in range(2):
            ag(0, p, direction).start()
    transpose_bc(0)

    def ag_step(k, _):
        for p in range(2):
            for direction in range(2):
                ag_wait(k - 1, p, direction)
                ag(k, p, direction).start()
        transpose_bc(k)
        return 0

    mid = max(1, half // 2)
    lax.fori_loop(1, mid, ag_step, 0)

    for n in range(2):
        for c in wx[n]:
            c.wait_recv()
    down_j = mod(x - 1, NX)
    up_j = mod(x + 1, NX)
    far_j = mod(x + 2, NX)
    fw_up = remote(wrow(xw, down_j), wrow(xw, down_j), ws.at[4], wr.at[4], x_up)
    fw_down = remote(wrow(zw, up_j), wrow(zw, up_j), ws.at[5], wr.at[5], x_down)
    fw_up.start()
    fw_down.start()
    sib = []
    for n, (buf, j) in enumerate(((zw, down_j), (zw, up_j), (xw, down_j), (xw, up_j), (zw, far_j), (xw, far_j))):
        sib.append(remote(wrow(buf, j), wrow(buf, j), sibs.at[n], sibr.at[n], sibling))
    for n in range(4):
        sib[n].start()

    lax.fori_loop(mid, half - 1, ag_step, 0)

    k_last = half - 1
    for p in range(2):
        for direction in range(2):
            ag_wait(k_last - 1, p, direction)
            if p == direction:
                ag(k_last, p, direction).start()
    transpose_bc(k_last)

    ow_up = remote(ow_in.at[half_in], wrow(ow, x), ws.at[6], wr.at[6], x_up)
    ow_down = remote(ow_in.at[half_in], wrow(ow, x), ws.at[7], wr.at[7], x_down)
    ow_up.start()
    ow_down.start()

    for c in small:
        c.wait_recv()
    swf[...] = jnp.zeros_like(swf)
    for r in range(nz):
        for j in range(NX):
            swf[j : j + 1, 128 * r : 128 * r + 128] = par[j, r : r + 1, :]
    low = lax.broadcasted_iota(jnp.int32, (8, 128), 1) < 64
    pt[...] = jnp.zeros_like(pt)
    for n in range(2):
        pair = jnp.where(low, par[2 * n, 16:24, :], par[2 * n + 1, 16:24, :])
        pt[0:8, 128 * n : 128 * n + 128] = pair
    pt[0:4, 256:512] = bck_in[...]
    ptt[...] = pt[...].T

    fw_up.wait_recv()
    fw_down.wait_recv()
    sib[4].start()
    sib[5].start()

    ag_wait(k_last, 0, 0)
    ag_wait(k_last, 1, 1)

    tokens = tok[...]
    step_raw = dot(swf[...].astype(BF16), tokens)
    xin[256:512, :] = dot(bct[...], tokens).astype(BF16)
    for c in sib:
        c.wait_recv()
    xin[0:256, :] = dot(xw[...], tokens).astype(BF16)

    pick_r = lax.broadcasted_iota(jnp.int32, (16, BLK), 0)
    pick_c = lax.broadcasted_iota(jnp.int32, (16, BLK), 1)
    pick = jnp.where((pick_c == pick_r + BLK - 3) & (pick_r < 3), 1.0, 0.0).astype(BF16)
    halo_s[...] = dot(pick, xin[...], BOTH).astype(BF16)
    halo = remote(halo_s, halo_r, hsem.at[0], hsem.at[1], next_dev)
    halo.start()

    ow_up.wait_recv()
    ow_down.wait_recv()

    def orow(j, part):
        return rows(ow, 64 * j + hr + 16 * part, 16)

    ofw_up = remote(orow(down_j, 0), orow(down_j, 0), ws.at[8], wr.at[8], x_up)
    ofw_down = remote(orow(up_j, 1), orow(up_j, 1), ws.at[9], wr.at[9], x_down)
    ofw_up.start()
    ofw_down.start()
    osib = []
    for n, j in enumerate((down_j, up_j, far_j)):
        osib.append(remote(wrow(ow, j), wrow(ow, j), sibs.at[6 + n], sibr.at[6 + n], sibling))
    osib[0].start()
    osib[1].start()

    def heads_col(r):
        col = jnp.concatenate([par[j, r : r + 1, :] for j in range(NX)] + [jnp.zeros((4, 128), F32)], axis=0)
        return jnp.concatenate([col, col], axis=1)

    arg = step_raw + heads_col(21)
    u = jnp.exp(-jnp.abs(arg))
    log1p = jnp.where(u < 0.02, u * (1.0 - u * (0.5 - u * (1.0 / 3.0 - u * (0.25 - u * 0.2)))), jnp.log(1.0 + u))
    step = jnp.maximum(arg, 0.0) + log1p
    rate = -jnp.exp(heads_col(22)) * step
    hi = rate.astype(BF16)
    rest = rate - hi.astype(F32)
    mid_part = rest.astype(BF16)
    lo = (rest - mid_part.astype(F32)).astype(BF16)
    ir = lax.broadcasted_iota(jnp.int32, (BLK, BLK), 0)
    ic = lax.broadcasted_iota(jnp.int32, (BLK, BLK), 1)
    tri = jnp.where(ir <= ic, 1.0, 0.0).astype(BF16)
    cum = dot(hi, tri) + dot(mid_part, tri) + dot(lo, tri)
    end = jnp.broadcast_to(cum[:, BLK - 1 : BLK], (8, BLK))
    tail = jnp.exp(end - cum) * step
    grow = jnp.exp(cum)
    tr[...] = jnp.zeros_like(tr)
    tr[0:8, :] = jnp.log(step) - cum
    col_t = tr[...].T

    z_in = dot(zw[...], tokens).astype(BF16).astype(F32)
    zsil[...] = z_in * jax.nn.sigmoid(z_in)

    halo.wait_recv()
    hrow = halo_r[...].astype(F32)
    k0, k1, k2 = pt[0:1, :], pt[1:2, :], pt[2:3, :]
    h0, h1, h2 = hrow[0:1], hrow[1:2], hrow[2:3]
    first = block > 0
    ct[...] = jnp.zeros_like(ct)
    ct[0:1, :] = jnp.where(first, k0 * h0 + k1 * h1 + k2 * h2, 0.0)
    ct[1:2, :] = jnp.where(first, k0 * h1 + k1 * h2, 0.0)
    ct[2:3, :] = jnp.where(first, k0 * h2, 0.0)
    shift = [jnp.where(ic == ir + d, 1.0, 0.0).astype(BF16) for d in range(1, 4)]
    for r in range(4):
        sl = slice(128 * r, 128 * r + 128)
        piece = xin[sl, :]
        taps = ptt[sl, :]
        total = taps[:, 3:4] * piece.astype(F32)
        for d in range(1, 4):
            total = total + taps[:, 3 - d : 4 - d] * dot(piece, shift[d - 1])
        corr = ct[:, sl].T
        total = jnp.concatenate([total[:, :128] + corr, total[:, 128:]], axis=1)
        total = total * jax.nn.sigmoid(total)
        if r < 2:
            xc[sl, :] = total.astype(BF16)
            for n in range(2):
                j = 2 * r + n
                wt[64 * j : 64 * j + 64, :] = (
                    total[64 * n : 64 * n + 64].astype(BF16).astype(F32) * tail[j : j + 1, :]
                ).astype(BF16)
        elif r == 2:
            b_rows = total.T.astype(BF16)
        else:
            c_cols = total.astype(BF16)

    loc = dot(wt[...], b_rows)
    for j in range(NX):
        st1s[j, 0:64, :] = loc[64 * j : 64 * j + 64]
        st1s[j, 64:72, :] = jnp.broadcast_to(end[j : j + 1, 0:128], (8, 128))
    st1r[x] = st1s[x]
    s1 = []
    for d in range(1, NX):
        xp = mod(x + d, NX)
        c = remote(st1s.at[xp], st1r.at[x], s1s.at[d - 1], s1r.at[d - 1], at(s, z, xp))
        c.start()
        s1.append(c)

    ofw_up.wait_recv()
    ofw_down.wait_recv()
    osib[2].start()

    gram = dot(b_rows, c_cols)
    lower = ir[:128, :128] <= ic[:128, :128]

    def intra(j):
        row = cum[j : j + 1, :]
        col = col_t[:, j : j + 1]
        d0 = jnp.where(lower, gram[:128, :128] * jnp.exp(row[:, :128] + col[:128]), 0.0).astype(BF16)
        full = (gram[:128, 128:] * jnp.exp(row[:, 128:] + col[:128])).astype(BF16)
        d1 = jnp.where(lower, gram[128:, 128:] * jnp.exp(row[:, 128:] + col[128:]), 0.0).astype(BF16)
        xj = xc[64 * j : 64 * j + 64, :]
        y0 = dot(xj[:, :128], d0)
        y1 = dot(xj, jnp.concatenate([full, d1], axis=0))
        skip = par[j, 23:24, :]
        y = jnp.concatenate([y0, y1], axis=1) + jnp.concatenate([skip, skip], axis=1) * xj.astype(F32)
        yv[64 * j : 64 * j + 64, :] = y

    intra(0)

    for c in s1:
        c.wait_recv()
    total_state = st1r[0, 0:64, :]
    total_log = st1r[0, 64:72, :]
    for q in range(1, NX):
        log_q = st1r[q, 64:72, :]
        total_state = jnp.exp(log_q[0:1]) * total_state + st1r[q, 0:64, :]
        total_log = total_log + log_q
    st2s[0:64, :] = total_state
    st2s[64:72, :] = total_log

    def s2(t):
        return remote(st2s, st2r.at[s], s2s.at[t - 1], s2r.at[s], (lax.rem(s + t, ns), h))

    for t in range(1, ns):

        @pl.when(s + t < ns)
        def _():
            s2(t).start()

    intra(1)
    intra(2)
    intra(3)

    def take(sp, carry):
        remote(st2s, st2r.at[sp], s2s.at[0], s2r.at[sp], (s, h)).wait_recv()
        factor = jnp.exp(st2r[sp, 64:65, :])
        return factor * carry + st2r[sp, 0:64, :]

    entering = lax.fori_loop(0, s, take, jnp.zeros((64, 128), F32))
    for q in range(NX):
        hs[q] = entering.astype(BF16)
        entering = jnp.exp(st1r[q, 64:65, :]) * entering + st1r[q, 0:64, :]
    held_own = rows(held, 64 * x, 64)
    s3 = []
    for d in range(1, NX):
        xp = mod(x + d, NX)
        c = remote(hs.at[xp], held_own, s3s.at[d - 1], s3r.at[d - 1], at(s, z, xp))
        c.start()
        s3.append(c)
    held[pl.ds(pl.multiple_of(64 * x, 64), 64), :] = hs[x]

    for c in osib:
        c.wait_recv()

    def transpose_ow(k, _):
        at_k = pl.ds(pl.multiple_of(BLK * k, BLK), BLK)
        owt[at_k, :] = ow[:, at_k].T
        return 0

    lax.fori_loop(0, half, transpose_ow, 0)

    for c in s3:
        c.wait_recv()

    square = jnp.zeros((8, BLK), F32)
    for j in range(NX):
        sl = slice(64 * j, 64 * j + 64)
        y = yv[sl, :] + grow[j : j + 1, :] * dot(held[sl, :], c_cols)
        gated = (y * zsil[sl, :]).astype(BF16).astype(F32)
        square = square + jnp.sum((gated * gated).reshape(8, 8, BLK), axis=0)
        sc[sl, :] = (gated * ptt[sl, 4:5]).astype(BF16)
    sqs[...] = jnp.sum(square, axis=0, keepdims=True)

    def partial(dest):
        return dot(owt[pl.ds(pl.multiple_of(128 * dest, 128), 128), :], sc[...])

    send_buf = (rs_rs, rs_ls)
    recv_buf = (rs_rr, rs_lr)

    def rs(k, p, direction):
        part = pl.ds(64 * p, 64)
        to = right if direction == 0 else left
        return remote(
            send_buf[direction].at[k, part],
            recv_buf[direction].at[k, part],
            rss.at[direction, k, p],
            rsr.at[direction, k, p],
            to,
        )

    def rs_dest(k, direction):
        return mod(z + half - k, nz) if direction == 0 else mod(z + nz - half + k, nz)

    for direction in range(2):
        p = direction
        own = partial(rs_dest(0, direction))
        send_buf[direction][0, 64 * p : 64 * p + 64, :] = own[64 * p : 64 * p + 64].astype(BF16)
        rs(0, p, direction).start()

    sq = []
    for d in range(1, nz):
        c = remote(sqs, sqr.at[d - 1], sqss.at[d - 1], sqrs.at[d - 1], at(s, mod(z + d, nz), x))
        c.start()
        sq.append(c)

    own = [partial(rs_dest(1, direction)) for direction in range(2)]
    for direction in range(2):
        p = 1 - direction
        send_buf[direction][1, 64 * p : 64 * p + 64, :] = own[direction][64 * p : 64 * p + 64].astype(BF16)
        rs(1, p, direction).start()
    for direction in range(2):
        p = direction
        rs(0, p, direction).wait_recv()
        got = recv_buf[direction][0, 64 * p : 64 * p + 64, :].astype(F32)
        send_buf[direction][1, 64 * p : 64 * p + 64, :] = (own[direction][64 * p : 64 * p + 64] + got).astype(BF16)
        rs(1, p, direction).start()

    def rs_step(k, _):
        own = [partial(rs_dest(k, direction)) for direction in range(2)]
        for n in range(2):
            for direction in range(2):
                p = (n + 1 - direction) % 2
                rs(k - 1, p, direction).wait_recv()
                part = slice(64 * p, 64 * p + 64)
                got = recv_buf[direction][k - 1, part, :].astype(F32)
                send_buf[direction][k, part, :] = (own[direction][part] + got).astype(BF16)
                rs(k, p, direction).start()
        return 0

    lax.fori_loop(2, half, rs_step, 0)

    own = partial(z)
    total_sq = sqs[...]
    for d in range(1, nz):
        sq[d - 1].wait_recv()
        total_sq = total_sq + sqr[d - 1]
    scale = lax.rsqrt(total_sq / (BLK * nz) + 1e-05)
    for n in range(2):
        for direction in range(2):
            rs(half - 1, (n + 1 - direction) % 2, direction).wait_recv()
    final = own + rs_rr[half - 1].astype(F32) + rs_lr[half - 1].astype(F32)
    res[...] = (final * scale).astype(BF16)

    p4 = []
    for d in range(1, NX):
        xp = mod(x + d, NX)
        c = remote(rows(res, 32 * xp, 32), out_ref.at[:, my_cols], p4s.at[d - 1], p4r.at[d - 1], at(s, z, xp))
        c.start()
        p4.append(c)
    keep = pltpu.make_async_copy(rows(res, 32 * x, 32), out_ref.at[:, my_cols], lsem.at[0])
    keep.start()

    for c in p1 + small + [c for pair in wx for c in pair] + [fw_up, fw_down] + sib:
        c.wait_send()
    for c in [ow_up, ow_down, ofw_up, ofw_down] + osib + [halo] + s1 + s3 + sq:
        c.wait_send()

    def ag_sent(k, _):
        for p in range(2):
            for direction in range(2):
                ag(k, p, direction).wait_send()
        return 0

    lax.fori_loop(0, half - 1, ag_sent, 0)
    for p in range(2):
        ag(half - 1, p, p).wait_send()
        rs(0, p, p).wait_send()

    def rs_sent(k, _):
        for p in range(2):
            for direction in range(2):
                rs(k, p, direction).wait_send()
        return 0

    lax.fori_loop(1, half, rs_sent, 0)
    for t in range(1, ns):

        @pl.when(s + t < ns)
        def _():
            s2(t).wait_send()

    for c in p4:
        c.wait()
    keep.wait()


def solution(mesh):
    ns = mesh.shape["seq"]
    nz = mesh.shape["head"] // NX
    half = nz // 2

    def body(tokens, z_weight, x_weight, bc_weight, step_weight, x_kernel, bc_kernel, step_bias, log_decay, skip_gain, norm_gain, out_weight):
        width = bc_weight.shape[0]
        vmem = pl.BlockSpec(memory_space=pltpu.VMEM)
        hbm = pl.BlockSpec(memory_space=pl.ANY)
        smem = pl.BlockSpec(memory_space=pltpu.SMEM)
        dma = pltpu.SemaphoreType.DMA

        def buf(*shape, dtype=BF16):
            return pltpu.VMEM(shape, dtype)

        out = pl.pallas_call(
            functools.partial(kernel, ns, nz),
            out_shape=jax.ShapeDtypeStruct((32, 4 * BLK), BF16),
            in_specs=[hbm, hbm, hbm, hbm, vmem, vmem, vmem, smem, smem, smem, vmem, hbm],
            out_specs=vmem,
            scratch_shapes=[
                buf(width, BLK),
                buf(256, width),
                buf(256, width),
                buf(width, 256),
                buf(256, width),
                buf(256, width),
                buf(width, 256),
                buf(NX, 24, 128, dtype=F32),
                buf(8, width, dtype=F32),
                buf(128, 512, dtype=F32),
                buf(512, 128, dtype=F32),
                buf(128, 512, dtype=F32),
                buf(512, BLK),
                buf(256, BLK, dtype=F32),
                buf(256, BLK),
                buf(16, 512),
                buf(16, 512),
                buf(128, BLK, dtype=F32),
                buf(16, 128, dtype=F32),
                buf(256, BLK),
                buf(256, BLK, dtype=F32),
                buf(NX, 72, 128, dtype=F32),
                buf(NX, 72, 128, dtype=F32),
                buf(72, 128, dtype=F32),
                buf(ns, 72, 128, dtype=F32),
                buf(NX, 64, 128),
                buf(256, 128),
                buf(1, BLK, dtype=F32),
                buf(nz - 1, 1, BLK, dtype=F32),
                buf(256, BLK),
                buf(half, 128, BLK),
                buf(half, 128, BLK),
                buf(half, 128, BLK),
                buf(half, 128, BLK),
                buf(128, BLK),
                dma((5,)),
                dma((3,)),
                dma((3,)),
                dma((10,)),
                dma((10,)),
                dma((9,)),
                dma((9,)),
                dma((3,)),
                dma((3,)),
                dma((2, half, 2)),
                dma((2, half, 2)),
                dma((2,)),
                dma((3,)),
                dma((3,)),
                dma((ns - 1,)),
                dma((ns,)),
                dma((3,)),
                dma((3,)),
                dma((nz - 1,)),
                dma((nz - 1,)),
                dma((2, half, 2)),
                dma((2, half, 2)),
                dma((3,)),
                dma((3,)),
            ],
            compiler_params=pltpu.CompilerParams(
                collective_id=0, has_side_effects=True, vmem_limit_bytes=40 * 1024 * 1024
            ),
        )(
            tokens.T,
            z_weight.T,
            x_weight.T,
            bc_weight,
            step_weight.T,
            x_kernel,
            bc_kernel,
            step_bias,
            log_decay,
            skip_gain,
            norm_gain.reshape(1, -1),
            out_weight,
        )
        return out.T

    return jax.shard_map(
        body,
        mesh=mesh,
        in_specs=(
            P("seq", "head"),
            P(None, "head"),
            P(None, "head"),
            P(),
            P(None, "head"),
            P(None, "head"),
            P(),
            P("head"),
            P("head"),
            P("head"),
            P("head"),
            P("head", None),
        ),
        out_specs=P("seq", "head"),
        check_vma=False,
    )
```

time: 404 us -> 103 us (0.25)
  the two profiles are of different devices: /device:TPU:10 before, /device:TPU:56 now
where the time goes in v1:
time: 103 us; the launch traced here: 102 us
  Pallas kernels  94.3 us (92%)
  local copies, waits for them, and re-layouts  6.21 us (6%)
  between operations  2 us (2%)
    pallas_call x1, Pallas kernels, body(): pl.pallas_call(functools.partial(kernel, ns, nz), out_shape=jax.ShapeDtyp...  94.3 us
    unnamed x19, local copies, waits for them, and re-layouts  6.21 us

profile of v1, /device:TPU:56, one launch (start us, length us, event | category | flops | bytes accessed | tf_op | source)
XLA Modules:
  0.0 102.5 jit_solution(2413261392108857315)
XLA Ops:
  0.0 0.0 copy-start.5
  2.0 0.0 copy-start.6
  2.0 0.0 copy-start.7
  2.0 0.0 copy-start.8
  2.0 0.0 copy-done.5
  2.0 0.6 copy-done.6
  2.6 0.0 copy-done.7
  2.7 0.0 copy-done.8
  2.7 0.0 copy-start
  2.7 1.2 %copy-done = bf16[2048,256]{1,0:T(8,128)(2,1)S(1)} copy-done((bf16[2048,256]{1,0:T(8,128)(2,1)S(1)}, bf16[2048,256]{1,0:T(8,128)(2,1)}, u32[]{:S(2)}) %copy-start) | copy-done | bytes 1048600
  3.9 0.0 copy-start.1
  3.9 0.9 copy-done.1
  4.8 0.0 copy-start.2
  4.8 0.9 copy-done.2
  5.8 0.0 copy-start.3
  5.8 0.9 copy-done.3
  6.7 0.0 copy-start.4
  6.7 0.8 copy-done.4
  7.6 94.3 %shard_map.118 = bf16[32,1024]{1,0:T(8,128)(2,1)S(1)} custom-call(bf16[32,1024]{1,0:T(8,128)(2,1)S(1)} %bitcast.9, bf16[64,2048]{1,0:T(8,128)(2,1)S(1)} %bitcast.6, bf16[64,2048]{1,0:T(8,128)(2,1)S(1)} %bitcast.7, bf16[2048,256]{1,0:T(8,128)(2,1)S(1)} %copy-done, bf16[1,2048]{1,0:T(2,128)(2,1)S(1)} %bitcast.10, f32[4,64]{1,0:T(4,128)S(1)} %copy-done.7, ...), custom_call_target="tpu_custom_call" | custom-call | tf_op jit(solution)/shard_map/pallas_call | solution.py:606
  101.9 0.6 copy.17
Async XLA Ops:
  0.0 2.0 %copy-start.5 = (bf16[2048,1]{0,1:T(2,128)(2,1)S(1)}, bf16[2048,1]{0,1:T(2,128)(2,1)}, u32[]{:S(2)}) copy-start(bf16[2048,1]{0,1:T(2,128)(2,1)} %param.16) | copy-start | bytes 12292
  2.0 0.7 copy-start.6
  2.0 0.7 copy-start.7
  2.0 0.7 copy-start.8
  2.7 1.2 %copy-start = (bf16[2048,256]{1,0:T(8,128)(2,1)S(1)}, bf16[2048,256]{1,0:T(8,128)(2,1)}, u32[]{:S(2)}) copy-start(bf16[2048,256]{1,0:T(8,128)(2,1)} %bcw_in.1) | copy-start | bytes 3145732
  3.9 0.9 copy-start.1
  4.8 0.9 copy-start.2
  5.8 0.9 copy-start.3
  6.7 0.8 copy-start.4

commit v2 on v1

--- a/solution.py
+++ b/solution.py
@@ -12,6 +12,7 @@
 BF16 = jnp.bfloat16
 NX = 4
 BLK = 256
+DELTAS = (2, -2, 1, -1, 0)
 NONE = (((1,), (0,)), ((), ()))
 BOTH = (((1,), (1,)), ((), ()))
 
@@ -66,11 +67,12 @@
     sqs,
     sqr,
     sc,
-    rs_rs,
-    rs_ls,
-    rs_rr,
-    rs_lr,
-    res,
+    sqt,
+    sqx,
+    rs_s,
+    rs_r,
+    fin_s,
+    fin_r,
     lsem,
     p1s,
     p1r,
@@ -91,10 +93,12 @@
     s3r,
     sqss,
     sqrs,
+    sqts,
+    sqtr,
     rss,
     rsr,
-    p4s,
-    p4r,
+    fins,
+    finr,
 ):
     half = nz // 2
     width = 128 * nz
@@ -112,8 +116,6 @@
     def mod(v, n):
         return lax.rem(v + n, n)
 
-    right = at(s, mod(z + 1, nz), x)
-    left = at(s, mod(z - 1, nz), x)
     x_up = at(s, z, mod(x + 1, NX))
     x_down = at(s, z, mod(x - 1, NX))
     sibling = (s + 1 - 2 * core, h)
@@ -147,9 +149,11 @@
     def greet(to):
         pl.semaphore_signal(barrier, inc=1, device_id=to, device_id_type=MESH)
 
-    for d in range(1, NX):
-        greet(at(s, z, mod(x + d, NX)))
-    for d in range(1, nz):
+    for delta in DELTAS:
+        for d in range(NX):
+            if (delta, d) != (0, 0):
+                greet(at(s, mod(z + delta, nz), mod(x + d, NX)))
+    for d in range(3, nz - 2):
         greet(at(s, mod(z + d, nz), x))
     for d in range(1, ns):
         greet((mod(s + d, ns), h))
@@ -168,15 +172,22 @@
     par[x, 22:23, :] = jnp.full((1, 128), decay_in[0], F32)
     par[x, 23:24, :] = jnp.full((1, 128), skip_in[0], F32)
 
-    pl.semaphore_wait(barrier, (NX - 1) + (nz - 1) + (ns - 1) + 2)
-
-    p1 = []
-    for d in range(1, NX):
+    pl.semaphore_wait(barrier, 5 * NX - 1 + (nz - 5) + (ns - 1) + 2)
+
+    def first(i, d):
         xp = mod(x + d, NX)
         cols = pl.ds(pl.multiple_of(BLK * xp, BLK), BLK)
-        c = remote(tok_in.at[:, cols], own_tok, p1s.at[d - 1], p1r.at[d - 1], at(s, z, xp))
+        to = at(s, mod(z + DELTAS[i], nz), xp)
+        return remote(tok_in.at[:, cols], own_tok, p1s.at[i, d], p1r.at[i, d], to)
+
+    def first_wait(i, xp):
+        d = mod(x - xp, NX)
+        ref = rows(tok, 128 * mod(z - DELTAS[i], nz) + 32 * xp, 32)
+        remote(ref, ref, p1s.at[i, d], p1r.at[i, d], x_up).wait_recv()
+
+    first_sends = [first(i, d) for i in range(5) for d in range(NX) if (DELTAS[i], d) != (0, 0)]
+    for c in first_sends:
         c.start()
-        p1.append(c)
     small = []
     for d in range(1, NX):
         c = remote(par.at[x], par.at[x], ps.at[d - 1], pr.at[d - 1], at(s, z, mod(x + d, NX)))
@@ -195,46 +206,68 @@
         down = remote(src.at[half_in], wrow(buf, x), ws.at[2 * n + 1], wr.at[2 * n + 1], x_down)
         wx.append((up, down))
 
-    for c in local:
-        c.wait()
-    for c in p1:
-        c.wait_recv()
+    def ag(k, p, direction, even):
+        sign = 1 - 2 * direction
+        ref = rows(tok, 128 * mod(z - 2 * sign * k, nz) + 64 * p, 64)
+        to = at(s, mod(z + sign * (1 + even), nz), x)
+        return remote(ref, ref, ags.at[direction, k, p, even], agr.at[direction, k, p, even], to)
+
+    def ag_wait(k, p, direction, even):
+        sign = 1 - 2 * direction
+        ref = rows(tok, 128 * mod(z - sign * (2 * k + 1 + even), nz) + 64 * p, 64)
+        remote(ref, ref, ags.at[direction, k, p, even], agr.at[direction, k, p, even], x_up).wait_recv()
+
+    def ag_has(k, p, direction, even):
+        return not even or 2 * k + 2 < half or p == direction
+
+    ag_sends = []
+
+    def ag_step(k):
+        for p in range(2):
+            for direction in range(2):
+                if k == 1:
+                    first_wait(direction, 2 * p)
+                    first_wait(direction, 2 * p + 1)
+                else:
+                    ag_wait(k - 1, p, direction, 1)
+                for even in (1, 0):
+                    if ag_has(k, p, direction, even):
+                        c = ag(k, p, direction, even)
+                        c.start()
+                        ag_sends.append(c)
+
+    def transpose_bc(k, _):
+        at_k = pl.ds(pl.multiple_of(BLK * k, BLK), BLK)
+        bct[:, at_k] = bcw[at_k, :].T
+        return 0
+
+    last = half // 2 - 1
+    local[1].wait()
+    lax.fori_loop(0, half // 2, transpose_bc, 0)
+    ag_step(1)
     wx[1][0].start()
     wx[0][1].start()
     wx[0][0].start()
     wx[1][1].start()
-
-    def ag(k, p, direction):
-        src = mod(z - k, nz) if direction == 0 else mod(z + k, nz)
-        ref = rows(tok, 128 * src + 64 * p, 64)
-        to = right if direction == 0 else left
-        return remote(ref, ref, ags.at[direction, k, p], agr.at[direction, k, p], to)
-
-    def ag_wait(k, p, direction):
-        src = mod(z - k - 1, nz) if direction == 0 else mod(z + k + 1, nz)
-        ref = rows(tok, 128 * src + 64 * p, 64)
-        remote(ref, ref, ags.at[direction, k, p], agr.at[direction, k, p], right).wait_recv()
-
-    def transpose_bc(k):
-        piece = bcw[pl.ds(pl.multiple_of(BLK * k, BLK), BLK), :]
-        bct[:, pl.ds(pl.multiple_of(BLK * k, BLK), BLK)] = piece.T
-
-    for p in range(2):
-        for direction in range(2):
-            ag(0, p, direction).start()
-    transpose_bc(0)
-
-    def ag_step(k, _):
-        for p in range(2):
-            for direction in range(2):
-                ag_wait(k - 1, p, direction)
-                ag(k, p, direction).start()
-        transpose_bc(k)
-        return 0
-
-    mid = max(1, half // 2)
-    lax.fori_loop(1, mid, ag_step, 0)
-
+    lax.fori_loop(half // 2, half, transpose_bc, 0)
+    for c in small:
+        c.wait_recv()
+    swf[...] = jnp.zeros_like(swf)
+    for r in range(nz):
+        for j in range(NX):
+            swf[j : j + 1, 128 * r : 128 * r + 128] = par[j, r : r + 1, :]
+    low = lax.broadcasted_iota(jnp.int32, (8, 128), 1) < 64
+    pt[...] = jnp.zeros_like(pt)
+    for n in range(2):
+        pair = jnp.where(low, par[2 * n, 16:24, :], par[2 * n + 1, 16:24, :])
+        pt[0:8, 128 * n : 128 * n + 128] = pair
+    pt[0:4, 256:512] = bck_in[...]
+    ptt[...] = pt[...].T
+    for k in range(2, last):
+        ag_step(k)
+
+    for n in (0, 2, 3, 4):
+        local[n].wait()
     for n in range(2):
         for c in wx[n]:
             c.wait_recv()
@@ -250,43 +283,30 @@
         sib.append(remote(wrow(buf, j), wrow(buf, j), sibs.at[n], sibr.at[n], sibling))
     for n in range(4):
         sib[n].start()
-
-    lax.fori_loop(mid, half - 1, ag_step, 0)
-
-    k_last = half - 1
-    for p in range(2):
-        for direction in range(2):
-            ag_wait(k_last - 1, p, direction)
-            if p == direction:
-                ag(k_last, p, direction).start()
-    transpose_bc(k_last)
+    if last > 1:
+        ag_step(last)
 
     ow_up = remote(ow_in.at[half_in], wrow(ow, x), ws.at[6], wr.at[6], x_up)
     ow_down = remote(ow_in.at[half_in], wrow(ow, x), ws.at[7], wr.at[7], x_down)
     ow_up.start()
     ow_down.start()
 
-    for c in small:
-        c.wait_recv()
-    swf[...] = jnp.zeros_like(swf)
-    for r in range(nz):
-        for j in range(NX):
-            swf[j : j + 1, 128 * r : 128 * r + 128] = par[j, r : r + 1, :]
-    low = lax.broadcasted_iota(jnp.int32, (8, 128), 1) < 64
-    pt[...] = jnp.zeros_like(pt)
-    for n in range(2):
-        pair = jnp.where(low, par[2 * n, 16:24, :], par[2 * n + 1, 16:24, :])
-        pt[0:8, 128 * n : 128 * n + 128] = pair
-    pt[0:4, 256:512] = bck_in[...]
-    ptt[...] = pt[...].T
-
     fw_up.wait_recv()
     fw_down.wait_recv()
     sib[4].start()
     sib[5].start()
 
-    ag_wait(k_last, 0, 0)
-    ag_wait(k_last, 1, 1)
+    for i in (2, 3):
+        for xp in range(NX):
+            first_wait(i, xp)
+    for d in range(1, NX):
+        first_wait(4, mod(x - d, NX))
+    for k in range(1, last + 1):
+        for p in range(2):
+            for direction in range(2):
+                ag_wait(k, p, direction, 0)
+                if k == last and ag_has(k, p, direction, 1):
+                    ag_wait(k, p, direction, 1)
 
     tokens = tok[...]
     step_raw = dot(swf[...].astype(BF16), tokens)
@@ -478,114 +498,115 @@
     def partial(dest):
         return dot(owt[pl.ds(pl.multiple_of(128 * dest, 128), 128), :], sc[...])
 
-    send_buf = (rs_rs, rs_ls)
-    recv_buf = (rs_rr, rs_lr)
-
-    def rs(k, p, direction):
+    def rs(m, p, direction, to):
         part = pl.ds(64 * p, 64)
-        to = right if direction == 0 else left
         return remote(
-            send_buf[direction].at[k, part],
-            recv_buf[direction].at[k, part],
-            rss.at[direction, k, p],
-            rsr.at[direction, k, p],
-            to,
+            rs_s.at[direction, m, part], rs_r.at[direction, m, part], rss.at[direction, m, p], rsr.at[direction, m, p], to
         )
 
-    def rs_dest(k, direction):
-        return mod(z + half - k, nz) if direction == 0 else mod(z + nz - half + k, nz)
-
-    for direction in range(2):
-        p = direction
-        own = partial(rs_dest(0, direction))
-        send_buf[direction][0, 64 * p : 64 * p + 64, :] = own[64 * p : 64 * p + 64].astype(BF16)
-        rs(0, p, direction).start()
-
+    rs_sends = []
+
+    def rs_start(m, p, direction):
+        step = 1 if m % 2 else 2
+        c = rs(m, p, direction, at(s, mod(z + (1 - 2 * direction) * step, nz), x))
+        c.start()
+        rs_sends.append(c)
+
+    def fin_start(i):
+        for d in range(NX):
+            if (DELTAS[i], d) != (0, 0):
+                xp = mod(x + d, NX)
+                src = fin_s.at[i, pl.ds(pl.multiple_of(32 * xp, 32), 32)]
+                c = remote(src, fin_r.at[i, d], fins.at[i, d], finr.at[i, d], at(s, mod(z + DELTAS[i], nz), xp))
+                c.start()
+                rs_sends.append(c)
+
+    def own(m, direction):
+        return partial(mod(z + (1 - 2 * direction) * m, nz))
+
+    def leaf(m):
+        for direction in range(2):
+            value = own(m, direction).astype(BF16)
+            if m == 1:
+                fin_s[2 + direction] = value
+                fin_start(2 + direction)
+                continue
+            rs_s[direction, m] = value
+            for p in range(2):
+                if m < half or p == direction:
+                    rs_start(m, p, direction)
+
+    leaf(half)
+    leaf(half - 1)
     sq = []
     for d in range(1, nz):
         c = remote(sqs, sqr.at[d - 1], sqss.at[d - 1], sqrs.at[d - 1], at(s, mod(z + d, nz), x))
         c.start()
         sq.append(c)
-
-    own = [partial(rs_dest(1, direction)) for direction in range(2)]
-    for direction in range(2):
-        p = 1 - direction
-        send_buf[direction][1, 64 * p : 64 * p + 64, :] = own[direction][64 * p : 64 * p + 64].astype(BF16)
-        rs(1, p, direction).start()
-    for direction in range(2):
-        p = direction
-        rs(0, p, direction).wait_recv()
-        got = recv_buf[direction][0, 64 * p : 64 * p + 64, :].astype(F32)
-        send_buf[direction][1, 64 * p : 64 * p + 64, :] = (own[direction][64 * p : 64 * p + 64] + got).astype(BF16)
-        rs(1, p, direction).start()
-
-    def rs_step(k, _):
-        own = [partial(rs_dest(k, direction)) for direction in range(2)]
-        for n in range(2):
+    leaf(half - 3)
+
+    mine = partial(z)
+    fin_s[4] = mine.astype(BF16)
+    sqt_sends = []
+    for m in range(half - 2, 0, -2):
+        values = [own(m, direction) for direction in range(2)]
+        for p in range(2):
+            part = slice(64 * p, 64 * p + 64)
             for direction in range(2):
-                p = (n + 1 - direction) % 2
-                rs(k - 1, p, direction).wait_recv()
-                part = slice(64 * p, 64 * p + 64)
-                got = recv_buf[direction][k - 1, part, :].astype(F32)
-                send_buf[direction][k, part, :] = (own[direction][part] + got).astype(BF16)
-                rs(k, p, direction).start()
-        return 0
-
-    lax.fori_loop(2, half, rs_step, 0)
-
-    own = partial(z)
-    total_sq = sqs[...]
-    for d in range(1, nz):
-        sq[d - 1].wait_recv()
-        total_sq = total_sq + sqr[d - 1]
-    scale = lax.rsqrt(total_sq / (BLK * nz) + 1e-05)
-    for n in range(2):
-        for direction in range(2):
-            rs(half - 1, (n + 1 - direction) % 2, direction).wait_recv()
-    final = own + rs_rr[half - 1].astype(F32) + rs_lr[half - 1].astype(F32)
-    res[...] = (final * scale).astype(BF16)
-
-    p4 = []
-    for d in range(1, NX):
-        xp = mod(x + d, NX)
-        c = remote(rows(res, 32 * xp, 32), out_ref.at[:, my_cols], p4s.at[d - 1], p4r.at[d - 1], at(s, z, xp))
-        c.start()
-        p4.append(c)
-    keep = pltpu.make_async_copy(rows(res, 32 * x, 32), out_ref.at[:, my_cols], lsem.at[0])
-    keep.start()
-
-    for c in p1 + small + [c for pair in wx for c in pair] + [fw_up, fw_down] + sib:
+                rs(m + 1, p, direction, x_up).wait_recv()
+                value = values[direction][part] + rs_r[direction, m + 1, part, :].astype(F32)
+                if m + 2 < half or p == direction:
+                    rs(m + 2, p, direction, x_up).wait_recv()
+                    value = value + rs_r[direction, m + 2, part, :].astype(F32)
+                if m > 2:
+                    rs_s[direction, m, part, :] = value.astype(BF16)
+                    rs_start(m, p, direction)
+                else:
+                    fin_s[direction, part, :] = value.astype(BF16)
+        if m == 2:
+            fin_start(0)
+            fin_start(1)
+        if m > 3:
+            leaf(m - 3)
+        if m == half - 2:
+            fin_start(4)
+            total_sq = sqs[...]
+            for d in range(1, nz):
+                sq[d - 1].wait_recv()
+                total_sq = total_sq + sqr[d - 1]
+            sqt[...] = total_sq
+            for d in range(1, NX):
+                c = remote(sqt, sqx.at[d - 1], sqts.at[d - 1], sqtr.at[d - 1], at(s, z, mod(x + d, NX)))
+                c.start()
+                sqt_sends.append(c)
+
+    for d in range(NX):
+        if d > 0:
+            sqt_sends[d - 1].wait_recv()
+            squares = sqx[d - 1]
+        else:
+            squares = sqt[...]
+        scale = lax.rsqrt(squares / (BLK * nz) + 1e-05)
+        if d == 0:
+            total = fin_s[4, pl.ds(pl.multiple_of(32 * x, 32), 32), :].astype(F32)
+        for i in (4, 2, 3, 0, 1):
+            if (DELTAS[i], d) != (0, 0):
+                ref = fin_r.at[i, d]
+                remote(ref, ref, fins.at[i, d], finr.at[i, d], x_up).wait_recv()
+                got = fin_r[i, d].astype(F32)
+                total = got if i == 4 else total + got
+        from_x = mod(x - d, NX)
+        out_ref[:, pl.ds(pl.multiple_of(BLK * from_x, BLK), BLK)] = (total * scale).astype(BF16)
+
+    for c in first_sends + small + [c for pair in wx for c in pair] + [fw_up, fw_down] + sib + ag_sends:
         c.wait_send()
-    for c in [ow_up, ow_down, ofw_up, ofw_down] + osib + [halo] + s1 + s3 + sq:
+    for c in [ow_up, ow_down, ofw_up, ofw_down] + osib + [halo] + s1 + s3 + sq + sqt_sends + rs_sends:
         c.wait_send()
-
-    def ag_sent(k, _):
-        for p in range(2):
-            for direction in range(2):
-                ag(k, p, direction).wait_send()
-        return 0
-
-    lax.fori_loop(0, half - 1, ag_sent, 0)
-    for p in range(2):
-        ag(half - 1, p, p).wait_send()
-        rs(0, p, p).wait_send()
-
-    def rs_sent(k, _):
-        for p in range(2):
-            for direction in range(2):
-                rs(k, p, direction).wait_send()
-        return 0
-
-    lax.fori_loop(1, half, rs_sent, 0)
     for t in range(1, ns):
 
         @pl.when(s + t < ns)
         def _():
             s2(t).wait_send()
-
-    for c in p4:
-        c.wait()
-    keep.wait()
 
 
 def solution(mesh):
@@ -639,22 +660,23 @@
                 buf(1, BLK, dtype=F32),
                 buf(nz - 1, 1, BLK, dtype=F32),
                 buf(256, BLK),
-                buf(half, 128, BLK),
-                buf(half, 128, BLK),
-                buf(half, 128, BLK),
-                buf(half, 128, BLK),
-                buf(128, BLK),
+                buf(1, BLK, dtype=F32),
+                buf(NX - 1, 1, BLK, dtype=F32),
+                buf(2, half + 1, 128, BLK),
+                buf(2, half + 1, 128, BLK),
+                buf(5, 128, BLK),
+                buf(5, NX, 32, BLK),
                 dma((5,)),
-                dma((3,)),
-                dma((3,)),
+                dma((5, NX)),
+                dma((5, NX)),
                 dma((10,)),
                 dma((10,)),
                 dma((9,)),
                 dma((9,)),
                 dma((3,)),
                 dma((3,)),
-                dma((2, half, 2)),
-                dma((2, half, 2)),
+                dma((2, half // 2, 2, 2)),
+                dma((2, half // 2, 2, 2)),
                 dma((2,)),
                 dma((3,)),
                 dma((3,)),
@@ -664,13 +686,15 @@
                 dma((3,)),
                 dma((nz - 1,)),
                 dma((nz - 1,)),
-                dma((2, half, 2)),
-                dma((2, half, 2)),
                 dma((3,)),
                 dma((3,)),
+                dma((2, half + 1, 2)),
+                dma((2, half + 1, 2)),
+                dma((5, NX)),
+                dma((5, NX)),
             ],
             compiler_params=pltpu.CompilerParams(
-                collective_id=0, has_side_effects=True, vmem_limit_bytes=40 * 1024 * 1024
+                collective_id=0, has_side_effects=True, vmem_limit_bytes=60 * 1024 * 1024
             ),
         )(
             tokens.T,

time: 103 us -> 82.2 us (0.80)
  the two profiles are of different devices: /device:TPU:56 before, /device:TPU:48 now
where the time goes in v2:
time: 82.2 us; the launch traced here: 82 us
  Pallas kernels  78.6 us (96%)
  between operations  1.95 us (2%)
  local copies, waits for them, and re-layouts  1.47 us (2%)
    pallas_call x1, Pallas kernels, body(): pl.pallas_call(functools.partial(kernel, ns, nz), out_shape=jax.ShapeDtyp...  78.6 us

profile of v2, /device:TPU:48, one launch (start us, length us, event | category | flops | bytes accessed | tf_op | source)
XLA Modules:
  0.0 82.0 jit_solution(1987748091353949689)
XLA Ops:
  1.9 78.6 %shard_map.118 = bf16[32,1024]{1,0:T(8,128)(2,1)} custom-call(bf16[32,1024]{1,0:T(8,128)(2,1)} %bitcast.9, bf16[64,2048]{1,0:T(8,128)(2,1)} %bitcast.6, bf16[64,2048]{1,0:T(8,128)(2,1)} %bitcast.7, bf16[2048,256]{1,0:T(8,128)(2,1)} %bcw_in.1, bf16[1,2048]{1,0:T(2,128)(2,1)} %bitcast.10, f32[4,64]{1,0:T(4,128)} %xk_in.1, f32[4,256]{1,0:T(4,128)} %bck_in.1, ...), custom_call_target="tpu_custom_call" | custom-call | tf_op jit(solution)/shard_map/pallas_call | solution.py:627
  80.5 1.5 %copy.17 = bf16[1024,32]{0,1:T(8,128)(2,1)} copy(bf16[1024,32]{0,1:T(8,128)(2,1)} %bitcast.8) | data formatting | bytes 131072

commit v3 on v2

--- a/solution.py
+++ b/solution.py
@@ -74,30 +74,22 @@
     fin_s,
     fin_r,
     lsem,
-    p1s,
+    snd,
     p1r,
-    ws,
+    p1x,
     wr,
-    sibs,
     sibr,
-    ps,
     pr,
-    ags,
     agr,
+    ago,
     hsem,
-    s1s,
     s1r,
-    s2s,
     s2r,
-    s3s,
     s3r,
-    sqss,
     sqrs,
-    sqts,
     sqtr,
-    rss,
     rsr,
-    fins,
+    rso,
     finr,
 ):
     half = nz // 2
@@ -124,10 +116,16 @@
     next_dev = at(after // NX, z, lax.rem(after, NX))
     prev_dev = at(before // NX, z, lax.rem(before, NX))
 
-    def remote(src, dst, send, recv, to):
+    def remote(src, dst, recv, to, group=0):
         return pltpu.make_async_remote_copy(
-            src_ref=src, dst_ref=dst, send_sem=send, recv_sem=recv, device_id=to, device_id_type=MESH
+            src_ref=src, dst_ref=dst, send_sem=snd.at[group], recv_sem=recv, device_id=to, device_id_type=MESH
         )
+
+    def wait_in(ref, sem):
+        remote(ref, ref, sem, sibling).wait_recv()
+
+    def wait_out(ref, group):
+        remote(ref, ref, hsem.at[0], sibling, group).wait_send()
 
     def rows(ref, start, count):
         return ref.at[pl.ds(pl.multiple_of(start, count), count)]
@@ -138,8 +136,8 @@
         pltpu.make_async_copy(tok_in.at[:, my_cols], own_tok, lsem.at[0]),
         pltpu.make_async_copy(bcw_in, bcw, lsem.at[1]),
         pltpu.make_async_copy(zw_in, rows(zw, 64 * x, 64), lsem.at[2]),
-        pltpu.make_async_copy(xw_in, rows(xw, 64 * x, 64), lsem.at[3]),
-        pltpu.make_async_copy(ow_in, rows(ow, 64 * x, 64), lsem.at[4]),
+        pltpu.make_async_copy(xw_in, rows(xw, 64 * x, 64), lsem.at[2]),
+        pltpu.make_async_copy(ow_in, rows(ow, 64 * x, 64), lsem.at[2]),
     ]
     for c in local:
         c.start()
@@ -178,19 +176,19 @@
         xp = mod(x + d, NX)
         cols = pl.ds(pl.multiple_of(BLK * xp, BLK), BLK)
         to = at(s, mod(z + DELTAS[i], nz), xp)
-        return remote(tok_in.at[:, cols], own_tok, p1s.at[i, d], p1r.at[i, d], to)
+        return remote(tok_in.at[:, cols], own_tok, p1r.at[i, d] if i < 2 else p1x.at[0], to)
 
     def first_wait(i, xp):
         d = mod(x - xp, NX)
         ref = rows(tok, 128 * mod(z - DELTAS[i], nz) + 32 * xp, 32)
-        remote(ref, ref, p1s.at[i, d], p1r.at[i, d], x_up).wait_recv()
+        remote(ref, ref, p1r.at[i, d] if i < 2 else p1x.at[0], x_up).wait_recv()
 
     first_sends = [first(i, d) for i in range(5) for d in range(NX) if (DELTAS[i], d) != (0, 0)]
     for c in first_sends:
         c.start()
     small = []
     for d in range(1, NX):
-        c = remote(par.at[x], par.at[x], ps.at[d - 1], pr.at[d - 1], at(s, z, mod(x + d, NX)))
+        c = remote(par.at[x], par.at[x], pr.at[0], at(s, z, mod(x + d, NX)), 5)
         c.start()
         small.append(c)
 
@@ -202,56 +200,70 @@
     half_in = pl.ds(pl.multiple_of(hr, 32), 32)
     wx = []
     for n, (src, buf) in enumerate(((zw_in, zw), (xw_in, xw))):
-        up = remote(src.at[half_in], wrow(buf, x), ws.at[2 * n], wr.at[2 * n], x_up)
-        down = remote(src.at[half_in], wrow(buf, x), ws.at[2 * n + 1], wr.at[2 * n + 1], x_down)
+        up = remote(src.at[half_in], wrow(buf, x), wr.at[0], x_up, 2)
+        down = remote(src.at[half_in], wrow(buf, x), wr.at[0], x_down, 2)
         wx.append((up, down))
+    wx[1][0].start()
+    wx[0][1].start()
+    wx[0][0].start()
+    wx[1][1].start()
+
+    last = half // 2 - 1
+
+    def ag_rows(k, p, even):
+        return (0, 128) if not even and k < last else (32 * p, 32)
+
+    def ag_sem(k, p, direction, even):
+        return agr.at[direction, k - 1, p] if even else ago.at[int(k == last)]
 
     def ag(k, p, direction, even):
         sign = 1 - 2 * direction
-        ref = rows(tok, 128 * mod(z - 2 * sign * k, nz) + 64 * p, 64)
+        start, count = ag_rows(k, p, even)
+        ref = rows(tok, 128 * mod(z - 2 * sign * k, nz) + start, count)
         to = at(s, mod(z + sign * (1 + even), nz), x)
-        return remote(ref, ref, ags.at[direction, k, p, even], agr.at[direction, k, p, even], to)
+        return remote(ref, ref, ag_sem(k, p, direction, even), to)
 
     def ag_wait(k, p, direction, even):
         sign = 1 - 2 * direction
-        ref = rows(tok, 128 * mod(z - sign * (2 * k + 1 + even), nz) + 64 * p, 64)
-        remote(ref, ref, ags.at[direction, k, p, even], agr.at[direction, k, p, even], x_up).wait_recv()
+        start, count = ag_rows(k, p, even)
+        ref = rows(tok, 128 * mod(z - sign * (2 * k + 1 + even), nz) + start, count)
+        remote(ref, ref, ag_sem(k, p, direction, even), x_up).wait_recv()
 
     def ag_has(k, p, direction, even):
-        return not even or 2 * k + 2 < half or p == direction
-
-    ag_sends = []
+        if even:
+            return k < last or p // 2 == direction
+        return k == last or p == 0
+
+    ag_pieces = []
 
     def ag_step(k):
-        for p in range(2):
+        for p in range(NX):
             for direction in range(2):
                 if k == 1:
-                    first_wait(direction, 2 * p)
-                    first_wait(direction, 2 * p + 1)
+                    first_wait(direction, p)
                 else:
                     ag_wait(k - 1, p, direction, 1)
                 for even in (1, 0):
-                    if ag_has(k, p, direction, even):
+                    if ag_has(k, p, direction, even) and (even or k == last):
                         c = ag(k, p, direction, even)
                         c.start()
-                        ag_sends.append(c)
+                        ag_pieces.append(1)
+        if k < last:
+            for direction in range(2):
+                c = ag(k, 0, direction, 0)
+                c.start()
+                ag_pieces.append(4)
 
     def transpose_bc(k, _):
         at_k = pl.ds(pl.multiple_of(BLK * k, BLK), BLK)
         bct[:, at_k] = bcw[at_k, :].T
         return 0
 
-    last = half // 2 - 1
     local[1].wait()
     lax.fori_loop(0, half // 2, transpose_bc, 0)
     ag_step(1)
-    wx[1][0].start()
-    wx[0][1].start()
-    wx[0][0].start()
-    wx[1][1].start()
     lax.fori_loop(half // 2, half, transpose_bc, 0)
-    for c in small:
-        c.wait_recv()
+    wait_in(par.at[pl.ds(0, NX - 1)], pr.at[0])
     swf[...] = jnp.zeros_like(swf)
     for r in range(nz):
         for j in range(NX):
@@ -266,75 +278,68 @@
     for k in range(2, last):
         ag_step(k)
 
-    for n in (0, 2, 3, 4):
-        local[n].wait()
-    for n in range(2):
-        for c in wx[n]:
-            c.wait_recv()
+    local[0].wait()
+    loaded = zw.at[pl.ds(0, 192)]
+    pltpu.make_async_copy(loaded, loaded, lsem.at[2]).wait()
+    wait_in(zw.at[pl.ds(0, 128)], wr.at[0])
     down_j = mod(x - 1, NX)
     up_j = mod(x + 1, NX)
     far_j = mod(x + 2, NX)
-    fw_up = remote(wrow(xw, down_j), wrow(xw, down_j), ws.at[4], wr.at[4], x_up)
-    fw_down = remote(wrow(zw, up_j), wrow(zw, up_j), ws.at[5], wr.at[5], x_down)
+    fw_up = remote(wrow(xw, down_j), wrow(xw, down_j), wr.at[1], x_up, 2)
+    fw_down = remote(wrow(zw, up_j), wrow(zw, up_j), wr.at[1], x_down, 2)
     fw_up.start()
     fw_down.start()
     sib = []
     for n, (buf, j) in enumerate(((zw, down_j), (zw, up_j), (xw, down_j), (xw, up_j), (zw, far_j), (xw, far_j))):
-        sib.append(remote(wrow(buf, j), wrow(buf, j), sibs.at[n], sibr.at[n], sibling))
+        sib.append(remote(wrow(buf, j), wrow(buf, j), sibr.at[0], sibling, 3))
     for n in range(4):
         sib[n].start()
     if last > 1:
         ag_step(last)
 
-    ow_up = remote(ow_in.at[half_in], wrow(ow, x), ws.at[6], wr.at[6], x_up)
-    ow_down = remote(ow_in.at[half_in], wrow(ow, x), ws.at[7], wr.at[7], x_down)
+    ow_up = remote(ow_in.at[half_in], wrow(ow, x), wr.at[2], x_up, 4)
+    ow_down = remote(ow_in.at[half_in], wrow(ow, x), wr.at[2], x_down, 4)
     ow_up.start()
     ow_down.start()
 
-    fw_up.wait_recv()
-    fw_down.wait_recv()
+    wait_in(zw.at[pl.ds(0, 64)], wr.at[1])
     sib[4].start()
     sib[5].start()
 
-    for i in (2, 3):
-        for xp in range(NX):
-            first_wait(i, xp)
-    for d in range(1, NX):
-        first_wait(4, mod(x - d, NX))
-    for k in range(1, last + 1):
-        for p in range(2):
-            for direction in range(2):
-                ag_wait(k, p, direction, 0)
-                if k == last and ag_has(k, p, direction, 1):
-                    ag_wait(k, p, direction, 1)
+    wait_in(tok.at[pl.ds(0, 32 * (3 * NX - 1))], p1x.at[0])
+    if last > 1:
+        wait_in(tok.at[pl.ds(0, 256 * (last - 1))], ago.at[0])
+    wait_in(tok.at[pl.ds(0, 256)], ago.at[1])
+    for p in range(NX):
+        for direction in range(2):
+            if ag_has(last, p, direction, 1):
+                ag_wait(last, p, direction, 1)
 
     tokens = tok[...]
     step_raw = dot(swf[...].astype(BF16), tokens)
     xin[256:512, :] = dot(bct[...], tokens).astype(BF16)
-    for c in sib:
-        c.wait_recv()
+    wait_in(zw.at[pl.ds(0, 192)], sibr.at[0])
     xin[0:256, :] = dot(xw[...], tokens).astype(BF16)
 
     pick_r = lax.broadcasted_iota(jnp.int32, (16, BLK), 0)
     pick_c = lax.broadcasted_iota(jnp.int32, (16, BLK), 1)
     pick = jnp.where((pick_c == pick_r + BLK - 3) & (pick_r < 3), 1.0, 0.0).astype(BF16)
     halo_s[...] = dot(pick, xin[...], BOTH).astype(BF16)
-    halo = remote(halo_s, halo_r, hsem.at[0], hsem.at[1], next_dev)
+    halo = remote(halo_s, halo_r, hsem.at[0], next_dev, 6)
     halo.start()
 
-    ow_up.wait_recv()
-    ow_down.wait_recv()
+    wait_in(ow.at[pl.ds(0, 64)], wr.at[2])
 
     def orow(j, part):
         return rows(ow, 64 * j + hr + 16 * part, 16)
 
-    ofw_up = remote(orow(down_j, 0), orow(down_j, 0), ws.at[8], wr.at[8], x_up)
-    ofw_down = remote(orow(up_j, 1), orow(up_j, 1), ws.at[9], wr.at[9], x_down)
+    ofw_up = remote(orow(down_j, 0), orow(down_j, 0), wr.at[3], x_up, 4)
+    ofw_down = remote(orow(up_j, 1), orow(up_j, 1), wr.at[3], x_down, 4)
     ofw_up.start()
     ofw_down.start()
     osib = []
     for n, j in enumerate((down_j, up_j, far_j)):
-        osib.append(remote(wrow(ow, j), wrow(ow, j), sibs.at[6 + n], sibr.at[6 + n], sibling))
+        osib.append(remote(wrow(ow, j), wrow(ow, j), sibr.at[1], sibling, 4))
     osib[0].start()
     osib[1].start()
 
@@ -405,12 +410,11 @@
     s1 = []
     for d in range(1, NX):
         xp = mod(x + d, NX)
-        c = remote(st1s.at[xp], st1r.at[x], s1s.at[d - 1], s1r.at[d - 1], at(s, z, xp))
+        c = remote(st1s.at[xp], st1r.at[x], s1r.at[0], at(s, z, xp), 7)
         c.start()
         s1.append(c)
 
-    ofw_up.wait_recv()
-    ofw_down.wait_recv()
+    wait_in(ow.at[pl.ds(0, 32)], wr.at[3])
     osib[2].start()
 
     gram = dot(b_rows, c_cols)
@@ -431,8 +435,7 @@
 
     intra(0)
 
-    for c in s1:
-        c.wait_recv()
+    wait_in(st1r.at[pl.ds(0, NX - 1)], s1r.at[0])
     total_state = st1r[0, 0:64, :]
     total_log = st1r[0, 64:72, :]
     for q in range(1, NX):
@@ -443,7 +446,7 @@
     st2s[64:72, :] = total_log
 
     def s2(t):
-        return remote(st2s, st2r.at[s], s2s.at[t - 1], s2r.at[s], (lax.rem(s + t, ns), h))
+        return remote(st2s, st2r.at[s], s2r.at[s], (lax.rem(s + t, ns), h), 10 + t)
 
     for t in range(1, ns):
 
@@ -456,7 +459,7 @@
     intra(3)
 
     def take(sp, carry):
-        remote(st2s, st2r.at[sp], s2s.at[0], s2r.at[sp], (s, h)).wait_recv()
+        remote(st2s, st2r.at[sp], s2r.at[sp], (s, h)).wait_recv()
         factor = jnp.exp(st2r[sp, 64:65, :])
         return factor * carry + st2r[sp, 0:64, :]
 
@@ -468,13 +471,12 @@
     s3 = []
     for d in range(1, NX):
         xp = mod(x + d, NX)
-        c = remote(hs.at[xp], held_own, s3s.at[d - 1], s3r.at[d - 1], at(s, z, xp))
+        c = remote(hs.at[xp], held_own, s3r.at[0], at(s, z, xp), 8)
         c.start()
         s3.append(c)
     held[pl.ds(pl.multiple_of(64 * x, 64), 64), :] = hs[x]
 
-    for c in osib:
-        c.wait_recv()
+    wait_in(ow.at[pl.ds(0, 96)], sibr.at[1])
 
     def transpose_ow(k, _):
         at_k = pl.ds(pl.multiple_of(BLK * k, BLK), BLK)
@@ -483,8 +485,7 @@
 
     lax.fori_loop(0, half, transpose_ow, 0)
 
-    for c in s3:
-        c.wait_recv()
+    wait_in(held.at[pl.ds(0, 192)], s3r.at[0])
 
     square = jnp.zeros((8, BLK), F32)
     for j in range(NX):
@@ -498,28 +499,33 @@
     def partial(dest):
         return dot(owt[pl.ds(pl.multiple_of(128 * dest, 128), 128), :], sc[...])
 
+    def whole(m):
+        return m % 2 == 1 and m < half - 1
+
     def rs(m, p, direction, to):
-        part = pl.ds(64 * p, 64)
-        return remote(
-            rs_s.at[direction, m, part], rs_r.at[direction, m, part], rss.at[direction, m, p], rsr.at[direction, m, p], to
-        )
-
-    rs_sends = []
+        part = pl.ds(0, 128) if whole(m) else pl.ds(32 * p, 32)
+        chain = (m - 1) // 2
+        sem = rso.at[direction, chain] if whole(m) else rsr.at[direction, chain, p]
+        return remote(rs_s.at[direction, m, part], rs_r.at[direction, m, part], sem, to, 1)
+
+    rs_pieces = []
 
     def rs_start(m, p, direction):
         step = 1 if m % 2 else 2
-        c = rs(m, p, direction, at(s, mod(z + (1 - 2 * direction) * step, nz), x))
+        rs(m, p, direction, at(s, mod(z + (1 - 2 * direction) * step, nz), x)).start()
+        rs_pieces.append(4 if whole(m) else 1)
+
+    def fin_piece(i, xp):
+        d = mod(xp - x, NX)
+        src = fin_s.at[i, pl.ds(pl.multiple_of(32 * xp, 32), 32)]
+        c = remote(src, fin_r.at[i, d], finr.at[d], at(s, mod(z + DELTAS[i], nz), xp), 1)
         c.start()
-        rs_sends.append(c)
+        rs_pieces.append(1)
 
     def fin_start(i):
         for d in range(NX):
             if (DELTAS[i], d) != (0, 0):
-                xp = mod(x + d, NX)
-                src = fin_s.at[i, pl.ds(pl.multiple_of(32 * xp, 32), 32)]
-                c = remote(src, fin_r.at[i, d], fins.at[i, d], finr.at[i, d], at(s, mod(z + DELTAS[i], nz), xp))
-                c.start()
-                rs_sends.append(c)
+                fin_piece(i, mod(x + d, NX))
 
     def own(m, direction):
         return partial(mod(z + (1 - 2 * direction) * m, nz))
@@ -532,15 +538,15 @@
                 fin_start(2 + direction)
                 continue
             rs_s[direction, m] = value
-            for p in range(2):
-                if m < half or p == direction:
+            for p in range(1 if whole(m) else NX):
+                if m < half or p // 2 == direction:
                     rs_start(m, p, direction)
 
     leaf(half)
     leaf(half - 1)
     sq = []
     for d in range(1, nz):
-        c = remote(sqs, sqr.at[d - 1], sqss.at[d - 1], sqrs.at[d - 1], at(s, mod(z + d, nz), x))
+        c = remote(sqs, sqr.at[d - 1], sqrs.at[0], at(s, mod(z + d, nz), x), 9)
         c.start()
         sq.append(c)
     leaf(half - 3)
@@ -550,58 +556,66 @@
     sqt_sends = []
     for m in range(half - 2, 0, -2):
         values = [own(m, direction) for direction in range(2)]
-        for p in range(2):
-            part = slice(64 * p, 64 * p + 64)
+        for p in range(NX):
+            part = slice(32 * p, 32 * p + 32)
             for direction in range(2):
-                rs(m + 1, p, direction, x_up).wait_recv()
+                if p == 0 and whole(m + 1):
+                    rs(m + 1, p, direction, x_up).wait_recv()
+                two = m + 2 < half or p // 2 == direction
+                both = two and not whole(m + 1)
+                if two or not whole(m + 1):
+                    wait_in(tok.at[pl.ds(0, 64 if both else 32)], rsr.at[direction, m // 2, p])
                 value = values[direction][part] + rs_r[direction, m + 1, part, :].astype(F32)
-                if m + 2 < half or p == direction:
-                    rs(m + 2, p, direction, x_up).wait_recv()
+                if two:
                     value = value + rs_r[direction, m + 2, part, :].astype(F32)
                 if m > 2:
                     rs_s[direction, m, part, :] = value.astype(BF16)
                     rs_start(m, p, direction)
                 else:
                     fin_s[direction, part, :] = value.astype(BF16)
-        if m == 2:
-            fin_start(0)
-            fin_start(1)
+                    fin_piece(direction, p)
         if m > 3:
             leaf(m - 3)
         if m == half - 2:
             fin_start(4)
             total_sq = sqs[...]
+            wait_in(sqr, sqrs.at[0])
             for d in range(1, nz):
-                sq[d - 1].wait_recv()
                 total_sq = total_sq + sqr[d - 1]
             sqt[...] = total_sq
             for d in range(1, NX):
-                c = remote(sqt, sqx.at[d - 1], sqts.at[d - 1], sqtr.at[d - 1], at(s, z, mod(x + d, NX)))
+                c = remote(sqt, sqx.at[d - 1], sqtr.at[0], at(s, z, mod(x + d, NX)), 10)
                 c.start()
                 sqt_sends.append(c)
 
+    wait_in(sqx, sqtr.at[0])
     for d in range(NX):
         if d > 0:
-            sqt_sends[d - 1].wait_recv()
             squares = sqx[d - 1]
         else:
             squares = sqt[...]
         scale = lax.rsqrt(squares / (BLK * nz) + 1e-05)
         if d == 0:
             total = fin_s[4, pl.ds(pl.multiple_of(32 * x, 32), 32), :].astype(F32)
+        wait_in(tok.at[pl.ds(0, 160 if d else 128)], finr.at[d])
         for i in (4, 2, 3, 0, 1):
             if (DELTAS[i], d) != (0, 0):
-                ref = fin_r.at[i, d]
-                remote(ref, ref, fins.at[i, d], finr.at[i, d], x_up).wait_recv()
                 got = fin_r[i, d].astype(F32)
                 total = got if i == 4 else total + got
         from_x = mod(x - d, NX)
         out_ref[:, pl.ds(pl.multiple_of(BLK * from_x, BLK), BLK)] = (total * scale).astype(BF16)
 
-    for c in first_sends + small + [c for pair in wx for c in pair] + [fw_up, fw_down] + sib + ag_sends:
-        c.wait_send()
-    for c in [ow_up, ow_down, ofw_up, ofw_down] + osib + [halo] + s1 + s3 + sq + sqt_sends + rs_sends:
-        c.wait_send()
+    wait_out(tok.at[pl.ds(0, 32 * (len(first_sends) + sum(ag_pieces)))], 0)
+    wait_out(tok.at[pl.ds(0, 32 * sum(rs_pieces))], 1)
+    wait_out(zw.at[pl.ds(0, 192)], 2)
+    wait_out(zw.at[pl.ds(0, 192)], 3)
+    wait_out(ow.at[pl.ds(0, 192)], 4)
+    wait_out(par.at[pl.ds(0, NX - 1)], 5)
+    wait_out(halo_s, 6)
+    wait_out(st1s.at[pl.ds(0, NX - 1)], 7)
+    wait_out(hs.at[pl.ds(0, NX - 1)], 8)
+    wait_out(sqr, 9)
+    wait_out(sqx, 10)
     for t in range(1, ns):
 
         @pl.when(s + t < ns)
@@ -617,7 +631,7 @@
     def body(tokens, z_weight, x_weight, bc_weight, step_weight, x_kernel, bc_kernel, step_bias, log_decay, skip_gain, norm_gain, out_weight):
         width = bc_weight.shape[0]
         vmem = pl.BlockSpec(memory_space=pltpu.VMEM)
-        hbm = pl.BlockSpec(memory_space=pl.ANY)
+        hbm = pl.BlockSpec(memory_space=pltpu.HBM)
         smem = pl.BlockSpec(memory_space=pltpu.SMEM)
         dma = pltpu.SemaphoreType.DMA
 
@@ -666,35 +680,27 @@
                 buf(2, half + 1, 128, BLK),
                 buf(5, 128, BLK),
                 buf(5, NX, 32, BLK),
-                dma((5,)),
-                dma((5, NX)),
-                dma((5, NX)),
-                dma((10,)),
-                dma((10,)),
-                dma((9,)),
-                dma((9,)),
                 dma((3,)),
-                dma((3,)),
-                dma((2, half // 2, 2, 2)),
-                dma((2, half // 2, 2, 2)),
+                dma((10 + ns,)),
+                dma((2, NX)),
+                dma((1,)),
+                dma((4,)),
                 dma((2,)),
-                dma((3,)),
-                dma((3,)),
-                dma((ns - 1,)),
+                dma((1,)),
+                dma((2, half // 2 - 1, NX)),
+                dma((2,)),
+                dma((1,)),
+                dma((1,)),
                 dma((ns,)),
-                dma((3,)),
-                dma((3,)),
-                dma((nz - 1,)),
-                dma((nz - 1,)),
-                dma((3,)),
-                dma((3,)),
-                dma((2, half + 1, 2)),
-                dma((2, half + 1, 2)),
-                dma((5, NX)),
-                dma((5, NX)),
+                dma((1,)),
+                dma((1,)),
+                dma((1,)),
+                dma((2, half // 2, NX)),
+                dma((2, half // 2)),
+                dma((NX,)),
             ],
             compiler_params=pltpu.CompilerParams(
-                collective_id=0, has_side_effects=True, vmem_limit_bytes=60 * 1024 * 1024
+                collective_id=0, has_side_effects=True, vmem_limit_bytes=(53 * 1024 + 880) * 1024
             ),
         )(
             tokens.T,

time: 82.2 us -> 78.6 us (0.956)
  the two profiles are of different devices: /device:TPU:48 before, /device:TPU:22 now
where the time goes in v3:
time: 78.6 us; the launch traced here: 78.3 us
  Pallas kernels  74.2 us (94%)
  local copies, waits for them, and re-layouts  2.14 us (3%)
  between operations  2 us (3%)
    pallas_call x1, Pallas kernels, body(): pl.pallas_call(functools.partial(kernel, ns, nz), out_shape=jax.ShapeDtyp...  74.2 us
    unnamed x9, local copies, waits for them, and re-layouts  2.14 us

profile of v3, /device:TPU:22, one launch (start us, length us, event | category | flops | bytes accessed | tf_op | source)
XLA Modules:
  0.0 78.3 jit_solution(17080697783286342643)
XLA Ops:
  0.0 0.0 copy-start
  2.0 0.0 copy-start.1
  2.0 0.0 copy-start.2
  2.0 0.0 copy-start.3
  2.0 0.0 copy-done
  2.0 0.6 copy-done.1
  2.6 0.0 copy-done.2
  2.7 0.0 copy-done.3
  2.7 74.2 %shard_map.118 = bf16[32,1024]{1,0:T(8,128)(2,1)} custom-call(bf16[32,1024]{1,0:T(8,128)(2,1)} %bitcast.11, bf16[64,2048]{1,0:T(8,128)(2,1)} %bitcast.8, bf16[64,2048]{1,0:T(8,128)(2,1)} %bitcast.9, bf16[2048,256]{1,0:T(8,128)(2,1)} %bcw_in.1, bf16[1,2048]{1,0:T(2,128)(2,1)S(1)} %bitcast.6, f32[4,64]{1,0:T(4,128)S(1)} %copy-done.2, f32[4,256]{1,0:T(4,128)S(1)} %copy-done.1, ...), custom_call_target="tpu_custom_call" | custom-call | tf_op jit(solution)/shard_map/pallas_call | solution.py:641
  76.8 1.5 %copy.17 = bf16[1024,32]{0,1:T(8,128)(2,1)} copy(bf16[1024,32]{0,1:T(8,128)(2,1)} %bitcast.10) | data formatting | bytes 131072
Async XLA Ops:
  0.0 2.0 %copy-start = (bf16[2048,1]{0,1:T(2,128)(2,1)S(1)}, bf16[2048,1]{0,1:T(2,128)(2,1)}, u32[]{:S(2)}) copy-start(bf16[2048,1]{0,1:T(2,128)(2,1)} %param.16) | copy-start | bytes 12292
  2.0 0.7 copy-start.1
  2.0 0.7 copy-start.2
  2.0 0.7 copy-start.3

commit v4 on v3

--- a/solution.py
+++ b/solution.py
@@ -130,6 +130,20 @@
     def rows(ref, start, count):
         return ref.at[pl.ds(pl.multiple_of(start, count), count)]
 
+    barrier = pltpu.get_barrier_semaphore()
+
+    def greet(to):
+        pl.semaphore_signal(barrier, inc=1, device_id=to, device_id_type=MESH)
+
+    for delta in DELTAS:
+        for d in range(NX):
+            if (delta, d) != (0, 0):
+                greet(at(s, mod(z + delta, nz), mod(x + d, NX)))
+    for d in range(1, ns):
+        greet((mod(s + d, ns), h))
+    greet(next_dev)
+    greet(prev_dev)
+
     own_tok = rows(tok, 128 * z + 32 * x, 32)
     my_cols = pl.ds(pl.multiple_of(BLK * x, BLK), BLK)
     local = [
@@ -142,22 +156,6 @@
     for c in local:
         c.start()
 
-    barrier = pltpu.get_barrier_semaphore()
-
-    def greet(to):
-        pl.semaphore_signal(barrier, inc=1, device_id=to, device_id_type=MESH)
-
-    for delta in DELTAS:
-        for d in range(NX):
-            if (delta, d) != (0, 0):
-                greet(at(s, mod(z + delta, nz), mod(x + d, NX)))
-    for d in range(3, nz - 2):
-        greet(at(s, mod(z + d, nz), x))
-    for d in range(1, ns):
-        greet((mod(s + d, ns), h))
-    greet(next_dev)
-    greet(prev_dev)
-
     par[x] = jnp.zeros((24, 128), F32)
     sw = sw_in[...].astype(F32)
     for r in range(nz):
@@ -170,7 +168,7 @@
     par[x, 22:23, :] = jnp.full((1, 128), decay_in[0], F32)
     par[x, 23:24, :] = jnp.full((1, 128), skip_in[0], F32)
 
-    pl.semaphore_wait(barrier, 5 * NX - 1 + (nz - 5) + (ns - 1) + 2)
+    pl.semaphore_wait(barrier, 5 * NX - 1 + (ns - 1) + 2)
 
     def first(i, d):
         xp = mod(x + d, NX)
@@ -635,12 +633,15 @@
         smem = pl.BlockSpec(memory_space=pltpu.SMEM)
         dma = pltpu.SemaphoreType.DMA
 
+        def pin(value):
+            return pltpu.with_memory_space_constraint(value, pltpu.HBM)
+
         def buf(*shape, dtype=BF16):
             return pltpu.VMEM(shape, dtype)
 
         out = pl.pallas_call(
             functools.partial(kernel, ns, nz),
-            out_shape=jax.ShapeDtypeStruct((32, 4 * BLK), BF16),
+            out_shape=pltpu.VMEM((32, 4 * BLK), BF16),
             in_specs=[hbm, hbm, hbm, hbm, vmem, vmem, vmem, smem, smem, smem, vmem, hbm],
             out_specs=vmem,
             scratch_shapes=[
@@ -700,13 +701,13 @@
                 dma((NX,)),
             ],
             compiler_params=pltpu.CompilerParams(
-                collective_id=0, has_side_effects=True, vmem_limit_bytes=(53 * 1024 + 880) * 1024
+                collective_id=0, has_side_effects=True, vmem_limit_bytes=40 * 1024 * 1024
             ),
         )(
-            tokens.T,
-            z_weight.T,
-            x_weight.T,
-            bc_weight,
+            pin(tokens.T),
+            pin(z_weight.T),
+            pin(x_weight.T),
+            pin(bc_weight),
             step_weight.T,
             x_kernel,
             bc_kernel,
@@ -714,7 +715,7 @@
             log_decay,
             skip_gain,
             norm_gain.reshape(1, -1),
-            out_weight,
+            pin(out_weight),
         )
         return out.T
 

time: 78.6 us -> 76 us (0.967)
  Pallas kernels: 74.2 us -> 72.5 us
  local copies, waits for them, and re-layouts: 2.14 us -> 1.3 us
    pallas_call x1, Pallas kernels: 74.2 us -> 72.5 us  [body(): pl.pallas_call(functools.partial(kernel, ns, nz), out_shape=pltpu.VMEM((3...]
    unnamed x9, local copies, waits for them, and re-layouts: 2.14 us -> 1.3 us
where the time goes in v4:
time: 76 us; the launch traced here: 75.8 us
  Pallas kernels  72.5 us (95%)
  between operations  2 us (3%)
  local copies, waits for them, and re-layouts  1.3 us (2%)
    pallas_call x1, Pallas kernels, body(): pl.pallas_call(functools.partial(kernel, ns, nz), out_shape=pltpu.VMEM((3...  72.5 us

profile of v4, /device:TPU:22, one launch (start us, length us, event | category | flops | bytes accessed | tf_op | source)
XLA Modules:
  0.0 75.8 jit_solution(16229325670514775117)
XLA Ops:
  0.0 0.0 copy-start
  2.0 0.0 copy-start.1
  2.0 0.0 copy-start.2
  2.0 0.0 copy-start.3
  2.0 0.0 copy-done
  2.0 0.6 copy-done.1
  2.6 0.0 copy-done.2
  2.7 0.0 copy-done.3
  2.7 72.5 %shard_map.118 = bf16[32,1024]{1,0:T(8,128)(2,1)S(1)} custom-call(bf16[32,1024]{1,0:T(8,128)(2,1)} %bitcast.11, bf16[64,2048]{1,0:T(8,128)(2,1)} %bitcast.9, bf16[64,2048]{1,0:T(8,128)(2,1)} %bitcast.10, bf16[2048,256]{1,0:T(8,128)(2,1)} %bcw_in.1, bf16[1,2048]{1,0:T(2,128)(2,1)S(1)} %bitcast.7, f32[4,64]{1,0:T(4,128)S(1)} %copy-done.2, ...), custom_call_target="tpu_custom_call" | custom-call | tf_op jit(solution)/shard_map/pallas_call | solution.py:642
  75.2 0.6 copy.14
Async XLA Ops:
  0.0 2.0 %copy-start = (bf16[2048,1]{0,1:T(2,128)(2,1)S(1)}, bf16[2048,1]{0,1:T(2,128)(2,1)}, u32[]{:S(2)}) copy-start(bf16[2048,1]{0,1:T(2,128)(2,1)} %param.16) | copy-start | bytes 12292
  2.0 0.7 copy-start.1
  2.0 0.7 copy-start.2
  2.0 0.7 copy-start.3

commit v5 on v4

--- a/solution.py
+++ b/solution.py
@@ -55,7 +55,7 @@
     halo_s,
     halo_r,
     tr,
-    bcv,
+    cv,
     wt,
     yv,
     st1s,
@@ -208,8 +208,11 @@
 
     last = half // 2 - 1
 
+    def piece(o):
+        return mod(x - (0, 1, 3, 2)[o], NX)
+
     def ag_rows(k, p, even):
-        return (0, 128) if not even and k < last else (32 * p, 32)
+        return (0, 128) if not even and k < last else (32 * piece(p), 32)
 
     def ag_sem(k, p, direction, even):
         return agr.at[direction, k - 1, p] if even else ago.at[int(k == last)]
@@ -238,7 +241,7 @@
         for p in range(NX):
             for direction in range(2):
                 if k == 1:
-                    first_wait(direction, p)
+                    first_wait(direction, piece(p))
                 else:
                     ag_wait(k - 1, p, direction, 1)
                 for even in (1, 0):
@@ -368,6 +371,17 @@
     z_in = dot(zw[...], tokens).astype(BF16).astype(F32)
     zsil[...] = z_in * jax.nn.sigmoid(z_in)
 
+    shift = [jnp.where(ic == ir + d, 1.0, 0.0).astype(BF16) for d in range(1, 4)]
+    for r in range(4):
+        sl = slice(128 * r, 128 * r + 128)
+        chunk = xin[sl, :]
+        taps = ptt[sl, :]
+        total = taps[:, 3:4] * chunk.astype(F32)
+        for d in range(1, 4):
+            total = total + taps[:, 3 - d : 4 - d] * dot(chunk, shift[d - 1])
+        after_border = total[:, 128:]
+        cv[sl, 0:128] = total[:, :128]
+        cv[sl, 128:256] = after_border * jax.nn.sigmoid(after_border)
     halo.wait_recv()
     hrow = halo_r[...].astype(F32)
     k0, k1, k2 = pt[0:1, :], pt[1:2, :], pt[2:3, :]
@@ -377,17 +391,10 @@
     ct[0:1, :] = jnp.where(first, k0 * h0 + k1 * h1 + k2 * h2, 0.0)
     ct[1:2, :] = jnp.where(first, k0 * h1 + k1 * h2, 0.0)
     ct[2:3, :] = jnp.where(first, k0 * h2, 0.0)
-    shift = [jnp.where(ic == ir + d, 1.0, 0.0).astype(BF16) for d in range(1, 4)]
     for r in range(4):
         sl = slice(128 * r, 128 * r + 128)
-        piece = xin[sl, :]
-        taps = ptt[sl, :]
-        total = taps[:, 3:4] * piece.astype(F32)
-        for d in range(1, 4):
-            total = total + taps[:, 3 - d : 4 - d] * dot(piece, shift[d - 1])
-        corr = ct[:, sl].T
-        total = jnp.concatenate([total[:, :128] + corr, total[:, 128:]], axis=1)
-        total = total * jax.nn.sigmoid(total)
+        border = cv[sl, 0:128] + ct[:, sl].T
+        total = jnp.concatenate([border * jax.nn.sigmoid(border), cv[sl, 128:256]], axis=1)
         if r < 2:
             xc[sl, :] = total.astype(BF16)
             for n in range(2):
@@ -663,7 +670,7 @@
                 buf(16, 512),
                 buf(16, 512),
                 buf(128, BLK, dtype=F32),
-                buf(16, 128, dtype=F32),
+                buf(512, BLK, dtype=F32),
                 buf(256, BLK),
                 buf(256, BLK, dtype=F32),
                 buf(NX, 72, 128, dtype=F32),

time: 76 us -> 74.2 us (0.976)
  Pallas kernels: 72.5 us -> 70.7 us
    pallas_call x1, Pallas kernels: 72.5 us -> 70.7 us  [body(): pl.pallas_call(functools.partial(kernel, ns, nz), out_shape=pltpu.VMEM((3...]
where the time goes in v5:
time: 74.2 us; the launch traced here: 74 us
  Pallas kernels  70.7 us (95%)
  between operations  2 us (3%)
  local copies, waits for them, and re-layouts  1.3 us (2%)
    pallas_call x1, Pallas kernels, body(): pl.pallas_call(functools.partial(kernel, ns, nz), out_shape=pltpu.VMEM((3...  70.7 us

profile of v5, /device:TPU:22, one launch (start us, length us, event | category | flops | bytes accessed | tf_op | source)
XLA Modules:
  0.0 74.0 jit_solution(12384231859731287069)
XLA Ops:
  0.0 0.0 copy-start
  2.0 0.0 copy-start.1
  2.0 0.0 copy-start.2
  2.0 0.0 copy-start.3
  2.0 0.0 copy-done
  2.0 0.6 copy-done.1
  2.6 0.0 copy-done.2
  2.7 0.0 copy-done.3
  2.7 70.7 %shard_map.118 = bf16[32,1024]{1,0:T(8,128)(2,1)S(1)} custom-call(bf16[32,1024]{1,0:T(8,128)(2,1)} %bitcast.11, bf16[64,2048]{1,0:T(8,128)(2,1)} %bitcast.9, bf16[64,2048]{1,0:T(8,128)(2,1)} %bitcast.10, bf16[2048,256]{1,0:T(8,128)(2,1)} %bcw_in.1, bf16[1,2048]{1,0:T(2,128)(2,1)S(1)} %bitcast.7, f32[4,64]{1,0:T(4,128)S(1)} %copy-done.2, ...), custom_call_target="tpu_custom_call" | custom-call | tf_op jit(solution)/shard_map/pallas_call | solution.py:649
  73.4 0.6 copy.14
Async XLA Ops:
  0.0 2.0 %copy-start = (bf16[2048,1]{0,1:T(2,128)(2,1)S(1)}, bf16[2048,1]{0,1:T(2,128)(2,1)}, u32[]{:S(2)}) copy-start(bf16[2048,1]{0,1:T(2,128)(2,1)} %param.16) | copy-start | bytes 12292
  2.0 0.7 copy-start.1
  2.0 0.7 copy-start.2
  2.0 0.7 copy-start.3

commit v6 on v5

--- a/solution.py
+++ b/solution.py
@@ -206,6 +206,11 @@
     wx[0][0].start()
     wx[1][1].start()
 
+    ow_up = remote(ow_in.at[half_in], wrow(ow, x), wr.at[2], x_up, 4)
+    ow_down = remote(ow_in.at[half_in], wrow(ow, x), wr.at[2], x_down, 4)
+    ow_up.start()
+    ow_down.start()
+
     last = half // 2 - 1
 
     def piece(o):
@@ -298,36 +303,9 @@
     if last > 1:
         ag_step(last)
 
-    ow_up = remote(ow_in.at[half_in], wrow(ow, x), wr.at[2], x_up, 4)
-    ow_down = remote(ow_in.at[half_in], wrow(ow, x), wr.at[2], x_down, 4)
-    ow_up.start()
-    ow_down.start()
-
     wait_in(zw.at[pl.ds(0, 64)], wr.at[1])
     sib[4].start()
     sib[5].start()
-
-    wait_in(tok.at[pl.ds(0, 32 * (3 * NX - 1))], p1x.at[0])
-    if last > 1:
-        wait_in(tok.at[pl.ds(0, 256 * (last - 1))], ago.at[0])
-    wait_in(tok.at[pl.ds(0, 256)], ago.at[1])
-    for p in range(NX):
-        for direction in range(2):
-            if ag_has(last, p, direction, 1):
-                ag_wait(last, p, direction, 1)
-
-    tokens = tok[...]
-    step_raw = dot(swf[...].astype(BF16), tokens)
-    xin[256:512, :] = dot(bct[...], tokens).astype(BF16)
-    wait_in(zw.at[pl.ds(0, 192)], sibr.at[0])
-    xin[0:256, :] = dot(xw[...], tokens).astype(BF16)
-
-    pick_r = lax.broadcasted_iota(jnp.int32, (16, BLK), 0)
-    pick_c = lax.broadcasted_iota(jnp.int32, (16, BLK), 1)
-    pick = jnp.where((pick_c == pick_r + BLK - 3) & (pick_r < 3), 1.0, 0.0).astype(BF16)
-    halo_s[...] = dot(pick, xin[...], BOTH).astype(BF16)
-    halo = remote(halo_s, halo_r, hsem.at[0], next_dev, 6)
-    halo.start()
 
     wait_in(ow.at[pl.ds(0, 64)], wr.at[2])
 
@@ -343,6 +321,28 @@
         osib.append(remote(wrow(ow, j), wrow(ow, j), sibr.at[1], sibling, 4))
     osib[0].start()
     osib[1].start()
+
+    wait_in(tok.at[pl.ds(0, 32 * (3 * NX - 1))], p1x.at[0])
+    if last > 1:
+        wait_in(tok.at[pl.ds(0, 256 * (last - 1))], ago.at[0])
+    wait_in(tok.at[pl.ds(0, 256)], ago.at[1])
+    for p in range(NX):
+        for direction in range(2):
+            if ag_has(last, p, direction, 1):
+                ag_wait(last, p, direction, 1)
+
+    tokens = tok[...]
+    step_raw = dot(swf[...].astype(BF16), tokens)
+    xin[256:512, :] = dot(bct[...], tokens).astype(BF16)
+    wait_in(zw.at[pl.ds(0, 192)], sibr.at[0])
+    xin[0:256, :] = dot(xw[...], tokens).astype(BF16)
+
+    pick_r = lax.broadcasted_iota(jnp.int32, (16, BLK), 0)
+    pick_c = lax.broadcasted_iota(jnp.int32, (16, BLK), 1)
+    pick = jnp.where((pick_c == pick_r + BLK - 3) & (pick_r < 3), 1.0, 0.0).astype(BF16)
+    halo_s[...] = dot(pick, xin[...], BOTH).astype(BF16)
+    halo = remote(halo_s, halo_r, hsem.at[0], next_dev, 6)
+    halo.start()
 
     def heads_col(r):
         col = jnp.concatenate([par[j, r : r + 1, :] for j in range(NX)] + [jnp.zeros((4, 128), F32)], axis=0)

time: 74.2 us -> 74 us (level)
  the two profiles are of different devices: /device:TPU:22 before, /device:TPU:54 now
where the time goes in v6:
time: 74 us; the launch traced here: 73.8 us
  Pallas kernels  70.5 us (95%)
  between operations  2 us (3%)
  local copies, waits for them, and re-layouts  1.3 us (2%)
    pallas_call x1, Pallas kernels, body(): pl.pallas_call(functools.partial(kernel, ns, nz), out_shape=pltpu.VMEM((3...  70.5 us

profile of v6, /device:TPU:54, one launch (start us, length us, event | category | flops | bytes accessed | tf_op | source)
XLA Modules:
  0.0 73.8 jit_solution(15049026654201161809)
XLA Ops:
  0.0 0.0 copy-start
  2.0 0.0 copy-start.1
  2.0 0.0 copy-start.2
  2.0 0.0 copy-start.3
  2.0 0.0 copy-done
  2.0 0.6 copy-done.1
  2.6 0.0 copy-done.2
  2.7 0.0 copy-done.3
  2.7 70.5 %shard_map.118 = bf16[32,1024]{1,0:T(8,128)(2,1)S(1)} custom-call(bf16[32,1024]{1,0:T(8,128)(2,1)} %bitcast.11, bf16[64,2048]{1,0:T(8,128)(2,1)} %bitcast.9, bf16[64,2048]{1,0:T(8,128)(2,1)} %bitcast.10, bf16[2048,256]{1,0:T(8,128)(2,1)} %bcw_in.1, bf16[1,2048]{1,0:T(2,128)(2,1)S(1)} %bitcast.7, f32[4,64]{1,0:T(4,128)S(1)} %copy-done.2, ...), custom_call_target="tpu_custom_call" | custom-call | tf_op jit(solution)/shard_map/pallas_call | solution.py:649
  73.1 0.6 copy.14
Async XLA Ops:
  0.0 2.0 %copy-start = (bf16[2048,1]{0,1:T(2,128)(2,1)S(1)}, bf16[2048,1]{0,1:T(2,128)(2,1)}, u32[]{:S(2)}) copy-start(bf16[2048,1]{0,1:T(2,128)(2,1)} %param.16) | copy-start | bytes 12292
  2.0 0.7 copy-start.1
  2.0 0.7 copy-start.2
  2.0 0.7 copy-start.3
